TPU v7x, 32 devices: a whole 2x2x4 slice. The times are simulated.
32 devices in a mesh: groups: 2 (over y), head: 4 (over z), req: 2 (over x), seq: 2 (over core).
Axes of the slice: x: 2, y: 2, z: 4, core: 2. Of those that a mesh axis runs over, the one named last changes fastest.
Arguments:
- queries: bfloat16 [4, 256, 6144], P(('groups', 'req'), 'seq', 'head'), parts along dimension 0, may hold values from -400 to 400
- hidden: bfloat16 [4, 256, 7168], P(('groups', 'req'), 'seq', 'head'), parts along dimension 0, may hold values from -6 to 6
- w_dkv: bfloat16 [7168, 576], P('head'), may hold values from -0.0625 to 0.0625
- kv_gain: float32 [512], replicated, may hold values from 0.1 to 1.9
- w_uk: bfloat16 [32, 128, 512], P('head'), may hold values from -0.5 to 0.5
- value_up_weight: bfloat16 [32, 512, 128], P('head'), may hold values from -0.25 to 0.25
- page_pool: bfloat16 [512, 36864], P(('groups', 'head', 'req')), parts along dimension 0, may hold values from -6 to 6
- page_owner: int32 [4, 64, 1], P('groups'), parts along dimension 0, may hold values from 0 to 7; in each aligned block of 64 rows (0 to 63, 64 to 127, ..., all dimensions but the last counted through in order) at most 16 rows name the same one
- page_slot: int32 [4, 64], P('groups'), parts along dimension 0, may hold values from 0 to 31
- prefix_len: int32 [4], P('groups'), parts along dimension 0, may hold values from 64 to 4096, as said below
- suffix_len: int32 [4], P('groups'), parts along dimension 0, may hold values from 128 to 256, as said below
Outputs:
- attn_out: bfloat16 [4, 256, 4096], P(('groups', 'req'), 'seq', 'head'), parts along dimension 0
- new_pages: bfloat16 [4, 4, 36864], P(('groups', 'req'), 'seq'), parts along dimension 0
There are 2 independent parts, one for each index of `groups`. A program takes and returns all parts, laid end to end along the dimension named above; an argument that names none is the same for every part. Nothing has to cross between parts.
Inputs may be any that keep to these rules, and one draw needn't show every extreme that they name: `page_owner`: in the rows of one request batch (1 request) no owner holds more than 16 pages, and some owner holds exactly 16. `prefix_len`: some request has the longest prefix. `suffix_len`: some request fills all suffix slots.
All inputs are finite; a program needn't handle non-finite values.
Results may differ from a plain program's by a relative error of at most 0.0055.
The roundings to bfloat16 on the way count: a program that leaves them out, or rounds other values in their place, can miss the bound.
Values may be sent and summed in bfloat16 or wider, within the bound.
No kernel may reach another device: no remote copies, remote signals or barrier semaphores. Data moves between devices by JAX's collectives and lax.ppermute only.
A program may use at most 128 MiB of HBM per device.

v0:
```python
import functools
import math

import jax
import jax.numpy as jnp
from jax import lax
from jax.experimental import pallas as pl
from jax.experimental.pallas import tpu as pltpu
from jax.sharding import PartitionSpec as P

LOWEST = -1e30
MASKED = -1e38
MIB = 1024 * 1024


def rotate(vector, cosine_table, sine_table):
    half_width = vector.shape[-1] // 2
    first_half = vector[..., :half_width]
    second_half = vector[..., half_width:]
    return jnp.concatenate(
        [
            first_half * cosine_table - second_half * sine_table,
            first_half * sine_table + second_half * cosine_table,
        ],
        axis=-1,
    )


def angles(positions, rope_width):
    half_width = rope_width // 2
    frequency = 10000.0 ** (-2.0 * jnp.arange(half_width, dtype=jnp.float32) / rope_width)
    phases = positions.astype(jnp.float32)[:, None] * frequency[None, :]
    return (jnp.cos(phases), jnp.sin(phases))


def finish_latent(summed, positions, live_rows, kv_gain, latent_width):
    latent_part = summed[:, :latent_width]
    mean_square = jnp.mean(latent_part * latent_part, axis=-1, keepdims=True)
    normed = latent_part * lax.rsqrt(mean_square + 1e-06) * kv_gain
    cosine_table, sine_table = angles(positions, summed.shape[1] - latent_width)
    rotated = rotate(summed[:, latent_width:], cosine_table, sine_table)
    joined = jnp.concatenate([normed, rotated], axis=-1).astype(jnp.bfloat16)
    return jnp.where(live_rows[:, None], joined, jnp.zeros_like(joined))


def any_spec():
    return pl.BlockSpec(memory_space=pl.ANY)


def smem_spec():
    return pl.BlockSpec(memory_space=pltpu.SMEM)


def vmem_spec():
    return pl.BlockSpec(memory_space=pltpu.VMEM)


def hbm_spec():
    return pl.BlockSpec(memory_space=pltpu.HBM)


def pick_kernel(
    cap, page_len, owner_hbm, slot_hbm, prefix_hbm, pool_hbm, hidden_hbm, down_hbm, count_ref, most_ref,
    first_ref, rest_ref, foreign_ref, partial_ref, owner_ref, slot_ref, prefix_ref, pool_ref, hidden_ref,
    down_ref, pages, lists, table, sems,
):
    n_req = lax.axis_size("req")
    head_idx = lax.axis_index("head")
    req_idx = lax.axis_index("req")
    seq_idx = lax.axis_index("seq")
    n_pages = owner_ref.shape[1]
    pool_pages, pairs, pair_width = pages.shape
    chunk = first_ref.shape[0]
    loads = [
        pltpu.make_async_copy(owner_hbm, owner_ref, sems.at[0]),
        pltpu.make_async_copy(slot_hbm, slot_ref, sems.at[1]),
        pltpu.make_async_copy(pool_hbm, pool_ref, sems.at[2]),
        pltpu.make_async_copy(hidden_hbm, hidden_ref, sems.at[6]),
        pltpu.make_async_copy(down_hbm, down_ref, sems.at[7]),
        pltpu.make_async_copy(prefix_hbm, prefix_ref, sems.at[8]),
    ]
    for load in loads:
        load.start()
    loads[0].wait()
    loads[1].wait()
    loads[5].wait()
    self_owner = head_idx * n_req + req_idx
    n_owners = table.shape[1]
    for shift in range(n_req):
        for owner in range(n_owners):
            table[shift, owner] = 0
    founds = []
    most = jnp.int32(0)
    for shift in range(n_req):
        request = lax.rem(req_idx + shift, n_req)

        def note(page, found, shift=shift, request=request):
            owner = owner_ref[request, page]
            needed = page * page_len < prefix_ref[request]
            table[shift, owner] += needed.astype(jnp.int32)
            lists[shift, found] = slot_ref[request, page]
            return found + (needed & (owner == self_owner)).astype(jnp.int32)

        founds.append(lax.fori_loop(0, n_pages, note, jnp.int32(0), unroll=8))
        for place in range(n_owners // n_req):
            held = functools.reduce(jnp.add, [table[shift, place * n_req + i] for i in range(n_req)])
            early = jnp.minimum(table[shift, place * n_req + request], chunk)
            most = jnp.maximum(most, held - early)
    for shift in range(n_req):
        count_ref[shift] = table[0, head_idx * n_req + lax.rem(req_idx + n_req - shift, n_req)]
    most_ref[0] = most
    loads[2].wait()
    step = 16
    row = lax.broadcasted_iota(jnp.int32, (step * step, step * step), 0)
    column = lax.broadcasted_iota(jnp.int32, (step * step, step * step), 1)
    swap = ((row // step == column % step) & (row % step == column // step)).astype(jnp.bfloat16)
    for page in range(0, pool_pages, step):
        for pair in range(0, pairs, step):
            rows = jnp.concatenate(
                [
                    pool_ref[page : page + step, (pair + i) * pair_width : (pair + i + 1) * pair_width]
                    for i in range(step)
                ],
                axis=0,
            )
            turned = jnp.dot(swap, rows, preferred_element_type=jnp.float32).astype(jnp.bfloat16)
            pages[page : page + step, pair : pair + step, :] = turned.reshape(step, step, pair_width)

    def send(shift, rank, target, sem):
        slot = jnp.where(rank < founds[shift], lists[shift, rank], 0)
        pltpu.make_async_copy(pages.at[slot], target, sem).start()

    for rank in range(cap):
        if rank < chunk:
            send(0, rank, first_ref.at[rank], sems.at[3])
        else:
            send(0, rank, rest_ref.at[rank - chunk], sems.at[4])
    half_cap = foreign_ref.shape[1]
    for shift in range(1, n_req):
        for j in range(half_cap):
            send(shift, seq_idx * half_cap + j, foreign_ref.at[shift - 1, j], sems.at[5])
    loads[3].wait()
    loads[4].wait()
    partial_ref[...] = lax.dot_general(
        hidden_ref[...], down_ref[...], (((1,), (1,)), ((), ())), preferred_element_type=jnp.float32
    )
    pltpu.make_async_copy(first_ref, first_ref, sems.at[3]).wait()
    if cap > chunk:
        pltpu.make_async_copy(rest_ref, rest_ref, sems.at[4]).wait()
    pltpu.make_async_copy(foreign_ref, foreign_ref, sems.at[5]).wait()


def pick_pages(
    page_owner, page_slot, prefix_len, page_pool, hidden, down, cap, chunk, n_head, n_req, n_seq, pairs
):
    pool_pages, page_width = page_pool.shape
    page = (pairs, page_width // pairs)
    return pl.pallas_call(
        functools.partial(pick_kernel, cap, 2 * pairs),
        out_shape=(
            jax.ShapeDtypeStruct((n_req,), jnp.int32),
            jax.ShapeDtypeStruct((1,), jnp.int32),
            jax.ShapeDtypeStruct((chunk, *page), jnp.bfloat16),
            jax.ShapeDtypeStruct((max(1, cap - chunk), *page), jnp.bfloat16),
            jax.ShapeDtypeStruct((n_req - 1, cap // n_seq, *page), jnp.bfloat16),
            jax.ShapeDtypeStruct((hidden.shape[0], down.shape[0]), jnp.float32),
        ),
        in_specs=[any_spec(), any_spec(), any_spec(), hbm_spec(), hbm_spec(), hbm_spec()],
        out_specs=(smem_spec(), smem_spec(), hbm_spec(), hbm_spec(), hbm_spec(), vmem_spec()),
        scratch_shapes=[
            pltpu.SMEM(page_owner.shape, jnp.int32),
            pltpu.SMEM(page_slot.shape, jnp.int32),
            pltpu.SMEM(prefix_len.shape, jnp.int32),
            pltpu.VMEM((pool_pages, page_width), jnp.bfloat16),
            pltpu.VMEM(hidden.shape, jnp.bfloat16),
            pltpu.VMEM(down.shape, jnp.bfloat16),
            pltpu.VMEM((pool_pages, *page), jnp.bfloat16),
            pltpu.SMEM((n_req, cap + 1), jnp.int32),
            pltpu.SMEM((n_req, n_head * n_req), jnp.int32),
            pltpu.SemaphoreType.DMA((9,)),
        ],
        compiler_params=pltpu.CompilerParams(vmem_limit_bytes=60 * MIB),
        cost_estimate=pl.CostEstimate(flops=10**9, bytes_accessed=6 * 10**6, transcendentals=0),
        name="pick_pages",
    )(page_owner, page_slot, prefix_len, page_pool, hidden, down)


def join_kernel(chunk, cap, count_ref, rest_ref, mine_ref, other_ref, *refs):
    n_req = count_ref.shape[0]
    targets, sems = refs[:-1], refs[-1]
    seq_idx = lax.axis_index("seq")
    half_cap = mine_ref.shape[1]
    excess = jnp.maximum(count_ref[0] - chunk, 0)
    j = 0
    for part, target in enumerate(targets):
        for place in range(target.shape[0]):

            def fetch(condition, source, target=target, place=place, part=part):
                @pl.when(condition)
                def _():
                    pltpu.make_async_copy(source, target.at[place], sems.at[part]).start()

            rank = jnp.int32(j)
            taken = rank < excess
            if cap > chunk:
                fetch(taken, rest_ref.at[jnp.minimum(rank, cap - chunk - 1)])
            rank = rank - excess
            for shift in range(1, n_req):
                here = jnp.logical_not(taken) & (rank < count_ref[shift])
                half = rank // half_cap
                slot = jnp.clip(rank - half * half_cap, 0, half_cap - 1)
                fetch(here & (half == seq_idx), mine_ref.at[shift - 1, slot])
                fetch(here & (half != seq_idx), other_ref.at[shift - 1, slot])
                taken = taken | here
                rank = rank - count_ref[shift]
            fetch(jnp.logical_not(taken), mine_ref.at[0, 0])
            j += 1
    for part, target in enumerate(targets):
        pltpu.make_async_copy(target, target, sems.at[part]).wait()


def join_pages(counts, rest, mine, other, chunk, cap, sizes):
    return pl.pallas_call(
        functools.partial(join_kernel, chunk, cap),
        out_shape=tuple(jax.ShapeDtypeStruct((size, *rest.shape[1:]), jnp.bfloat16) for size in sizes),
        in_specs=[smem_spec()] + [hbm_spec()] * 3,
        out_specs=(vmem_spec(),) * len(sizes),
        scratch_shapes=[pltpu.SemaphoreType.DMA((len(sizes),))],
        compiler_params=pltpu.CompilerParams(vmem_limit_bytes=10 * MIB),
        cost_estimate=pl.CostEstimate(flops=0, bytes_accessed=3 * 10**6, transcendentals=0),
        name="join_pages",
    )(counts, rest, mine, other)


def token_limits(owners, prefix, req_idx, n_head, n_req, chunk, slots, page_len):
    pages = owners.shape[0]
    order = jnp.arange(pages, dtype=jnp.int32)
    place = owners // n_req
    shift = lax.rem(req_idx + n_req - lax.rem(owners, n_req), n_req)
    key = shift * pages + order
    together = (place[None, :] == place[:, None]) & (order * page_len < prefix)[None, :]
    rank = jnp.sum((together & (key[None, :] < key[:, None])).astype(jnp.int32), axis=1)
    held = jnp.sum((together & (shift[None, :] == 0)).astype(jnp.int32), axis=1)
    early = (shift == 0) & (rank < chunk)
    within = jnp.where(early, rank, chunk + rank - jnp.minimum(held, chunk))
    slot = place * slots + within
    tokens = jnp.clip(prefix - order * page_len, 0, page_len)
    all_slots = jnp.arange(n_head * slots, dtype=jnp.int32)
    limits = jnp.sum(jnp.where(slot[None, :] == all_slots[:, None], tokens[None, :], 0), axis=1)
    return limits.reshape(n_head, slots)


def over_groups(most):
    n_groups = lax.axis_size("groups")
    passed = most
    for _ in range(n_groups - 1):
        passed = lax.ppermute(passed, "groups", [(i, (i + 1) % n_groups) for i in range(n_groups)])
        most = jnp.maximum(most, passed)
    return most[0]


def query_kernel(query_ref, up_ref, cosine_ref, sine_ref, out_ref):
    heads, nope_width, latent_width = up_ref.shape
    half_len, width = query_ref.shape
    query_width = width // heads
    half_rope = cosine_ref.shape[0]
    key_width = latent_width + 2 * half_rope
    for head in range(heads):
        part = slice(head * half_len, (head + 1) * half_len)
        both = query_ref[:, head * query_width : (head + 1) * query_width]
        latent = lax.dot_general(
            up_ref[head], both[:, :nope_width], (((0,), (1,)), ((), ())), preferred_element_type=jnp.float32
        )
        out_ref[:latent_width, part] = latent.astype(jnp.bfloat16)
        turned = both[:, nope_width:].astype(jnp.float32).T
        low, high = turned[:half_rope], turned[half_rope:]
        out_ref[latent_width : latent_width + half_rope, part] = (
            low * cosine_ref[...] - high * sine_ref[...]
        ).astype(jnp.bfloat16)
        out_ref[latent_width + half_rope : key_width, part] = (
            low * sine_ref[...] + high * cosine_ref[...]
        ).astype(jnp.bfloat16)
    rest = out_ref.shape[0] - key_width
    row = lax.broadcasted_iota(jnp.int32, (rest, out_ref.shape[1]), 0)
    out_ref[key_width:, :] = (row == 0).astype(jnp.bfloat16)


def turn_queries(queries, w_uk, cosine_table, sine_table, key_rows):
    heads, nope_width, latent_width = w_uk.shape
    rows = heads * queries.shape[0]
    return pl.pallas_call(
        query_kernel,
        out_shape=jax.ShapeDtypeStruct((key_rows, rows), jnp.bfloat16),
        in_specs=[vmem_spec()] * 4,
        out_specs=vmem_spec(),
        compiler_params=pltpu.CompilerParams(vmem_limit_bytes=20 * MIB),
        cost_estimate=pl.CostEstimate(
            flops=2 * rows * nope_width * latent_width, bytes_accessed=3 * 10**6, transcendentals=0
        ),
        name="turn_queries",
    )(queries, w_uk, cosine_table, sine_table)


def score_block(keys, queries_ref, target, note, highest, weight_sum, tile, scale, bias=None):
    rows = queries_ref.shape[1]
    for start in range(0, rows, tile):
        part = slice(start, start + tile)
        scores = jnp.dot(keys[...], queries_ref[:, part], preferred_element_type=jnp.float32) * scale
        if bias is not None:
            scores = scores + bias
        old = highest[:, part]
        new = jnp.maximum(old, jnp.max(scores, axis=0, keepdims=True))
        weights = jnp.exp2(scores - new)
        highest[:, part] = new
        weight_sum[:, part] = weight_sum[:, part] * jnp.exp2(old - new) + jnp.sum(
            weights, axis=0, keepdims=True
        )
        target[:, part] = weights
        note(part, new)


def block_limits(limit_ref, block, chunk):
    return [limit_ref[block * chunk + j] for j in range(chunk)]


def any_token(limit_ref, block, chunk):
    return functools.reduce(jnp.maximum, block_limits(limit_ref, block, chunk)) > 0


def load_block(block_ref, keys, limits, key_width):
    chunk, pairs, pair_width = block_ref.shape
    pair_rows = chunk * pairs
    page_rows = block_ref[...].reshape(pair_rows, pair_width)
    keys[:pair_rows, :key_width] = page_rows[:, :key_width]
    keys[pair_rows:, :key_width] = page_rows[:, key_width:]
    shape = (2 * pair_rows, keys.shape[1] - key_width)
    row = lax.broadcasted_iota(jnp.int32, shape, 0)
    pair_row = lax.rem(row, pair_rows)
    token = 2 * lax.rem(pair_row, pairs) + row // pair_rows
    limit = jnp.zeros_like(row)
    for j, value in enumerate(limits):
        limit = jnp.where(pair_row // pairs == j, value, limit)
    masked = (lax.broadcasted_iota(jnp.int32, shape, 1) == 0) & (token >= limit)
    keys[:, key_width:] = jnp.where(masked, MASKED, 0.0).astype(jnp.bfloat16)


def turn_values(keys, latent_width):
    return keys[:, :latent_width].T


def near_bias(n_keys, half_len, tile, live):
    seq_idx = lax.axis_index("seq")
    place = lax.broadcasted_iota(jnp.int32, (n_keys, tile), 0)
    query = lax.rem(lax.broadcasted_iota(jnp.int32, (n_keys, tile), 1), half_len) + seq_idx * half_len
    allowed = (place <= query) & (place < live)
    return jnp.where(allowed, 0.0, -jnp.inf)


def score_kernel(shape, base, n_sources, first, near, limit_ref, queries_ref, *refs):
    tile, scale, chunk, key_width = shape
    refs = list(refs)
    if not first:
        marks_in, sum_in, high_in = [refs.pop(0) for _ in range(3)]
        refs.pop(0), refs.pop(0)
    if near:
        live_ref, suffix_ref = refs.pop(0), refs.pop(0)
    sources = [refs.pop(0) for _ in range(n_sources)]
    weights_hbm, values_hbm, marks, weight_sum, highest = [refs.pop(0) for _ in range(5)]
    if near:
        near_weights, near_values, near_mark = [refs.pop(0) for _ in range(3)]
    blocks, keys, weights, values, load_sems, weight_sems, value_sems = [refs.pop(0) for _ in range(7)]
    n_blocks = blocks.shape[0]
    latent_width = values.shape[1]
    index = 0
    for source in sources:
        for i in range(source.shape[0] // chunk):
            pltpu.make_async_copy(
                source.at[i * chunk : (i + 1) * chunk], blocks.at[index], load_sems.at[index]
            ).start()
            index += 1
    if first:
        marks[...] = jnp.zeros_like(marks)
        weight_sum[...] = jnp.zeros_like(weight_sum)
        highest[...] = jnp.full_like(highest, LOWEST)
    else:
        marks[...] = marks_in[...]
        weight_sum[...] = sum_in[...]
        highest[...] = high_in[...]

    def stores(block):
        return (
            pltpu.make_async_copy(weights.at[block], weights_hbm.at[base + block], weight_sems.at[block]),
            pltpu.make_async_copy(values.at[block], values_hbm.at[base + block], value_sems.at[block]),
        )

    def one_block(block, carry):
        pltpu.make_async_copy(blocks.at[block], blocks.at[block], load_sems.at[block]).wait()

        @pl.when(any_token(limit_ref, block, chunk))
        def _():
            load_block(blocks.at[block], keys, block_limits(limit_ref, block, chunk), key_width)

            def note(part, new):
                marks[pl.ds(base + block, 1), part] = new

            score_block(
                keys, queries_ref, weights.at[block], note, highest, weight_sum, tile, scale
            )
            values[block] = turn_values(keys, latent_width)
            for copy in stores(block):
                copy.start()

        return carry

    lax.fori_loop(0, n_blocks, one_block, 0)
    if near:
        near_keys = refs.pop(0)
        n_near = suffix_ref.shape[0]
        near_keys[:, key_width:] = jnp.zeros_like(near_keys[:, key_width:])
        near_keys[:, :key_width] = suffix_ref[...]

        def note_near(part, new):
            near_mark[:, part] = new

        score_block(
            near_keys, queries_ref, near_weights, note_near, highest, weight_sum, tile, scale,
            near_bias(n_near, n_near // lax.axis_size("seq"), tile, live_ref[0]),
        )
        near_values[...] = turn_values(near_keys, latent_width)

    def one_wait(block, carry):
        @pl.when(any_token(limit_ref, block, chunk))
        def _():
            for copy in stores(block):
                copy.wait()

        return carry

    lax.fori_loop(0, n_blocks, one_wait, 0)


def score_part(base, total, limits, queries, sources, state, shape, latent_width, near=None):
    tile, scale, chunk, key_width = shape
    width, rows = queries.shape
    _, pairs, pair_width = sources[0].shape
    block_keys = 2 * chunk * pairs
    n_blocks = sum(s.shape[0] for s in sources) // chunk
    row = jax.ShapeDtypeStruct((1, rows), jnp.float32)
    out_shape = [
        jax.ShapeDtypeStruct((total, block_keys, rows), jnp.float32),
        jax.ShapeDtypeStruct((total, latent_width, block_keys), jnp.bfloat16),
        jax.ShapeDtypeStruct((total, rows), jnp.float32),
        row,
        row,
    ]
    out_specs = [hbm_spec(), hbm_spec(), vmem_spec(), vmem_spec(), vmem_spec()]
    operands = [limits, queries]
    specs = [smem_spec(), vmem_spec()]
    aliases = {}
    if state is not None:
        operands += [state[2], state[3], state[4], state[0], state[1]]
        specs += [vmem_spec()] * 3 + [hbm_spec()] * 2
        aliases = {5: 0, 6: 1}
    scratch = [
        pltpu.VMEM((n_blocks, chunk, pairs, pair_width), jnp.bfloat16),
        pltpu.VMEM((block_keys, width), jnp.bfloat16),
        pltpu.VMEM((n_blocks, block_keys, rows), jnp.float32),
        pltpu.VMEM((n_blocks, latent_width, block_keys), jnp.bfloat16),
        pltpu.SemaphoreType.DMA((n_blocks,)),
        pltpu.SemaphoreType.DMA((n_blocks,)),
        pltpu.SemaphoreType.DMA((n_blocks,)),
    ]
    if near is not None:
        near_keys = near[-1].shape[0]
        operands += list(near)
        specs += [smem_spec(), vmem_spec()]
        out_shape += [
            jax.ShapeDtypeStruct((near_keys, rows), jnp.float32),
            jax.ShapeDtypeStruct((latent_width, near_keys), jnp.bfloat16),
            row,
        ]
        out_specs += [vmem_spec()] * 3
        scratch.append(pltpu.VMEM((near_keys, width), jnp.bfloat16))
    operands += list(sources)
    specs += [hbm_spec()] * len(sources)
    work = n_blocks * block_keys * rows // 2
    return pl.pallas_call(
        functools.partial(score_kernel, shape, base, len(sources), state is None, near is not None),
        out_shape=tuple(out_shape),
        in_specs=specs,
        out_specs=tuple(out_specs),
        scratch_shapes=scratch,
        input_output_aliases=aliases,
        compiler_params=pltpu.CompilerParams(vmem_limit_bytes=40 * MIB),
        cost_estimate=pl.CostEstimate(
            flops=work, bytes_accessed=10**5, transcendentals=0
        ),
        name="score_part",
    )(*operands)


def finish_kernel(
    shape, depth, n_blocks, n_sources, limit_ref, last_limit_ref, queries_ref, marks, sum_in, high_in,
    near_weights, near_values, near_mark, live_ref, up_ref, weights_hbm, values_hbm, *refs,
):
    tile, scale, chunk, key_width = shape
    sources, refs = refs[:n_sources], refs[n_sources:]
    (
        out_ref, weight_sum, highest, total, blocks, keys, last_weights, last_values, last_marks,
        weights, values, used, load_sems, weight_sems, value_sems,
    ) = refs
    rows = queries_ref.shape[1]
    latent_width = total.shape[0]
    n_last = blocks.shape[0]
    index = 0
    for source in sources:
        for i in range(source.shape[0] // chunk):
            pltpu.make_async_copy(
                source.at[i * chunk : (i + 1) * chunk], blocks.at[index], load_sems.at[index]
            ).start()
            index += 1

    def list_block(block, count):
        used[count] = block
        return count + any_token(limit_ref, block, chunk).astype(jnp.int32)

    n_used = lax.fori_loop(0, n_blocks, list_block, jnp.int32(0))

    def fetches(number):
        place = lax.rem(number, depth)
        return (
            pltpu.make_async_copy(weights_hbm.at[used[number]], weights.at[place], weight_sems.at[place]),
            pltpu.make_async_copy(values_hbm.at[used[number]], values.at[place], value_sems.at[place]),
        )

    def fetch(number):
        @pl.when(number < n_used)
        def _():
            for copy in fetches(number):
                copy.start()

    for number in range(depth):
        fetch(jnp.int32(number))
    weight_sum[...] = sum_in[...]
    highest[...] = high_in[...]
    last_marks[...] = jnp.zeros_like(last_marks)

    def one_score(block, carry):
        pltpu.make_async_copy(blocks.at[block], blocks.at[block], load_sems.at[block]).wait()

        @pl.when(any_token(last_limit_ref, block, chunk))
        def _():
            load_block(blocks.at[block], keys, block_limits(last_limit_ref, block, chunk), key_width)

            def note(part, new):
                last_marks[pl.ds(block, 1), part] = new

            score_block(
                keys, queries_ref, last_weights.at[block], note, highest, weight_sum, tile, scale
            )
            last_values[block] = turn_values(keys, latent_width)

        return carry

    lax.fori_loop(0, n_last, one_score, 0)

    def add_block(weight_block, value_block, mark, begin=False):
        for start in range(0, rows, tile):
            part = slice(start, start + tile)
            factor = jnp.exp2(mark[:, part] - highest[:, part]) / weight_sum[:, part]
            added = jnp.dot(
                value_block[...],
                (weight_block[:, part] * factor).astype(jnp.bfloat16),
                preferred_element_type=jnp.float32,
            )
            total[:, part] = added if begin else total[:, part] + added

    add_block(near_weights, near_values, near_mark, begin=True)

    def one_add(number, carry):
        for copy in fetches(number):
            copy.wait()
        place = lax.rem(number, depth)
        add_block(weights.at[place], values.at[place], marks.at[pl.ds(used[number], 1)])
        fetch(number + depth)
        return carry

    lax.fori_loop(0, n_used, one_add, 0)

    def one_last(block, carry):
        @pl.when(any_token(last_limit_ref, block, chunk))
        def _():
            add_block(last_weights.at[block], last_values.at[block], last_marks.at[pl.ds(block, 1)])

        return carry

    lax.fori_loop(0, n_last, one_last, 0)
    heads, _, value_width = up_ref.shape
    half_len = out_ref.shape[0]
    steps = lax.broadcasted_iota(jnp.int32, (half_len, value_width), 0)
    steps = steps + lax.axis_index("seq") * half_len
    for head in range(heads):
        latent = total[:, head * half_len : (head + 1) * half_len].astype(jnp.bfloat16)
        raised = lax.dot_general(
            latent, up_ref[head], (((0,), (0,)), ((), ())), preferred_element_type=jnp.float32
        )
        out_ref[:, head * value_width : (head + 1) * value_width] = jnp.where(
            steps < live_ref[0], raised, 0.0
        ).astype(jnp.bfloat16)


def finish(n_blocks, limits, last_limits, queries, state, near_state, sources, live, up_weight, half_len, shape):
    tile, scale, chunk, key_width = shape
    weights, values, marks, weight_sum, highest = state
    width, rows = queries.shape
    _, latent_width, block_keys = values.shape
    _, pairs, pair_width = sources[0].shape
    heads, _, value_width = up_weight.shape
    depth = 4
    n_last = sum(s.shape[0] for s in sources) // chunk
    row = pltpu.VMEM((1, rows), jnp.float32)
    work = (n_blocks // 2 + n_last) * block_keys * rows
    return pl.pallas_call(
        functools.partial(finish_kernel, shape, depth, n_blocks, len(sources)),
        out_shape=jax.ShapeDtypeStruct((half_len, heads * value_width), jnp.bfloat16),
        in_specs=[smem_spec()] * 2
        + [vmem_spec()] * 7
        + [smem_spec(), vmem_spec()]
        + [hbm_spec()] * (2 + len(sources)),
        out_specs=vmem_spec(),
        scratch_shapes=[
            row,
            row,
            pltpu.VMEM((latent_width, rows), jnp.float32),
            pltpu.VMEM((n_last, chunk, pairs, pair_width), jnp.bfloat16),
            pltpu.VMEM((block_keys, width), jnp.bfloat16),
            pltpu.VMEM((n_last, block_keys, rows), jnp.float32),
            pltpu.VMEM((n_last, latent_width, block_keys), jnp.bfloat16),
            pltpu.VMEM((n_last, rows), jnp.float32),
            pltpu.VMEM((depth, block_keys, rows), jnp.float32),
            pltpu.VMEM((depth, latent_width, block_keys), jnp.bfloat16),
            pltpu.SMEM((n_blocks + depth + 1,), jnp.int32),
            pltpu.SemaphoreType.DMA((n_last,)),
            pltpu.SemaphoreType.DMA((depth,)),
            pltpu.SemaphoreType.DMA((depth,)),
        ],
        compiler_params=pltpu.CompilerParams(vmem_limit_bytes=40 * MIB),
        cost_estimate=pl.CostEstimate(
            flops=2 * work * latent_width, bytes_accessed=3 * 10**7, transcendentals=work // 4
        ),
        name="finish",
    )(
        limits, last_limits, queries, marks, weight_sum, highest, *near_state, live, up_weight,
        weights, values, *sources,
    )


def local(
    queries,
    hidden,
    w_dkv,
    kv_gain,
    w_uk,
    value_up_weight,
    page_pool,
    page_owner,
    page_slot,
    prefix_len,
    suffix_len,
):
    n_head = lax.axis_size("head")
    n_req = lax.axis_size("req")
    n_seq = lax.axis_size("seq")
    head_idx = lax.axis_index("head")
    req_idx = lax.axis_index("req")
    seq_idx = lax.axis_index("seq")
    _, half_len, d_local = hidden.shape
    heads_dev, nope_width, latent_width = w_uk.shape
    lat_width = w_dkv.shape[1]
    rope_width = lat_width - latent_width
    query_width = queries.shape[2] // heads_dev
    page_width = page_pool.shape[1]
    page_len = page_width // lat_width
    pairs = page_len // 2
    pages_req = page_slot.shape[1]
    cap = max(2, 2 * pages_req // (n_head * n_req))
    chunk = n_req * cap // 4
    slots = 4 * chunk
    score_scale = float(query_width) ** (-0.5)

    owner_rows = page_owner[:, :, 0]
    counts, most, first, rest, foreign, partial_value = pick_pages(
        owner_rows, page_slot, prefix_len, page_pool, hidden[0], w_dkv.T,
        cap, chunk, n_head, n_req, n_seq, pairs,
    )
    swap_route = [(i, n_seq - 1 - i) for i in range(n_seq)]
    stream_route = []
    for i in range(n_head - 1):
        stream_route.append((i * n_seq, (i + 1) * n_seq))
        stream_route.append(((i + 1) * n_seq + 1, i * n_seq + 1))

    def swap(block):
        return lax.ppermute(block, "seq", swap_route)

    def stream(block):
        return lax.ppermute(block, ("head", "seq"), stream_route)

    my_prefix = lax.dynamic_index_in_dim(prefix_len, req_idx, 0, keepdims=False)
    my_suffix = lax.dynamic_index_in_dim(suffix_len, req_idx, 0, keepdims=False)
    own_owners = lax.dynamic_index_in_dim(owner_rows, req_idx, 0, keepdims=False)
    place_limits = token_limits(own_owners, my_prefix, req_idx, n_head, n_req, chunk, slots, page_len)
    upward = 2 * seq_idx - 1
    origins = [head_idx]
    for step in range(1, n_head):
        origins += [head_idx + upward * step, head_idx - upward * step]
    origins = jnp.stack(origins)
    heads = jnp.arange(n_head, dtype=jnp.int32)
    limits = jnp.sum(
        jnp.where((origins[:, None] == heads[None, :])[:, :, None], place_limits[None], 0), axis=1
    )

    positions = my_prefix + seq_idx * half_len + jnp.arange(half_len, dtype=jnp.int32)
    rows = heads_dev * half_len
    half_rope = rope_width // 2
    frequency = 10000.0 ** (-2.0 * jnp.arange(half_rope, dtype=jnp.float32) / rope_width)
    phases = frequency[:, None] * positions.astype(jnp.float32)[None, :]
    q_turned = turn_queries(queries[0], w_uk, jnp.cos(phases), jnp.sin(phases), lat_width + 64)

    arrived = [
        lax.ppermute(foreign[s - 1], "req", [(i, (i + s) % n_req) for i in range(n_req)])
        for s in range(1, n_req)
    ]
    early_steps = [stream(first)]
    share = half_len // n_head
    partials = lax.all_to_all(partial_value, "head", split_axis=0, concat_axis=0, tiled=True)
    summed = jnp.sum(partials.reshape(n_head, share, lat_width), axis=0)
    share_t = seq_idx * half_len + head_idx * share + jnp.arange(share, dtype=jnp.int32)
    latent = finish_latent(summed, my_prefix + share_t, share_t < my_suffix, kv_gain, latent_width)
    copies = jnp.concatenate([latent] * n_head, axis=0)
    fresh = lax.all_to_all(copies, "head", split_axis=0, concat_axis=0, tiled=True)
    early_steps[0], fresh = lax.optimization_barrier((early_steps[0], fresh))
    for step in range(1, n_head - 1):
        early_steps.append(stream(early_steps[-1]))
    early_steps = [[block, None] for block in early_steps]
    for step in range(n_head - 2):
        early_steps[step][1] = swap(early_steps[step][0])
    mine = arrived[0][None] if n_req == 2 else jnp.stack(arrived)
    mine, fresh = lax.optimization_barrier((mine, fresh))
    other = swap(mine)
    middle, late = join_pages(counts, rest, mine, other, chunk, cap, (2 * chunk, chunk))

    tile = 256 if rows % 256 == 0 and 256 % half_len == 0 else half_len
    shape = (tile, score_scale * math.log2(math.e), chunk, lat_width)
    parts = {"early": (0, chunk), "middle": (chunk, 3 * chunk), "late": (3 * chunk, 4 * chunk)}

    def limits_of(pieces):
        return jnp.concatenate(
            [limits[origin, parts[name][0] : parts[name][1]] for name, origin in pieces]
        )

    def pieces_of(name, steps):
        return [(name, 2 * step + side + 1) for step in steps for side in range(2)]

    def arrays_of(arrived_steps, steps):
        return [arrived_steps[step][side] for step in steps for side in range(2)]

    last = n_head - 2
    live = my_suffix.reshape(1)
    near_state = ()
    extra = 4 + 1 + 2 * last
    total = 1 + 2 * (last + 1) + 2 + 4 * last + extra
    used_limits = []
    n_blocks = 0
    state = None

    def score(pieces, arrays, near=None):
        nonlocal n_blocks, state, near_state
        used_limits.append(limits_of(pieces))
        result = score_part(
            n_blocks, total, used_limits[-1], q_turned, arrays, state, shape, latent_width, near
        )
        state = result[:5]
        near_state = result[5:] or near_state
        n_blocks += sum(a.shape[0] for a in arrays) // chunk

    def tie(block):
        nonlocal state
        block, mark = lax.optimization_barrier((block, state[4]))
        state = (*state[:4], mark)
        return block

    middle, early_steps[last - 1][0] = lax.optimization_barrier((middle, early_steps[last - 1][0]))
    middle_steps = []
    block = stream(middle)
    for step in range(last + 1):
        received = block
        if step == 0:
            score(
                [("early", 0)] + pieces_of("early", range(last)),
                [first] + arrays_of(early_steps, range(last)),
            )
        elif step == 1:
            score(
                pieces_of("early", [last]) + [("middle", 0)] + pieces_of("middle", [0]),
                arrays_of(early_steps, [last]) + [middle] + arrays_of(middle_steps, [0]),
            )
        else:
            score(
                pieces_of("middle", [step - 1]),
                arrays_of(middle_steps, [step - 1]),
                (live, suffix_latent) if step == last else None,
            )
        received = tie(received)
        if step == 0:
            early_steps[last][0] = tie(early_steps[last][0])
            early_steps[last][1] = swap(early_steps[last][0])
            opposite = swap(fresh)
            suffix_latent = jnp.where(
                seq_idx == 0,
                jnp.concatenate([fresh, opposite], axis=0),
                jnp.concatenate([opposite, fresh], axis=0),
            )
            most = over_groups(most)
            received, most = lax.optimization_barrier((received, most))
        elif step == last - 1:
            received, suffix_latent = lax.optimization_barrier((received, suffix_latent))
        if step < last:
            block = stream(received)
        middle_steps.append([received, swap(received)])

    last_pieces = pieces_of("middle", [last])
    last_arrays = arrays_of(middle_steps, [last])

    known = jnp.concatenate(used_limits)
    final = limits_of(last_pieces)

    def end(blocks, blocks_limits, final_limits, final_arrays, current):
        return finish(
            blocks, blocks_limits, final_limits, q_turned, current, near_state,
            final_arrays, live, value_up_weight, half_len, shape,
        )

    def with_late(_):
        block = stream(late)
        pieces = last_pieces + [("late", 0)]
        arrays = last_arrays + [late]
        current, blocks, limit_list = state, n_blocks, list(used_limits)
        for step in range(last + 1):
            received = block
            more = limits_of(pieces)
            limit_list.append(more)
            current = score_part(
                blocks, total, more, q_turned, arrays, current, shape, latent_width
            )[:5]
            blocks += sum(a.shape[0] for a in arrays) // chunk
            received, mark = lax.optimization_barrier((received, current[4]))
            current = (*current[:4], mark)
            if step < last:
                block = stream(received)
            arrays = [received, swap(received)]
            pieces = pieces_of("late", [step])
        return end(blocks, jnp.concatenate(limit_list), limits_of(pieces), arrays, current)

    def without_late(_):
        return end(n_blocks, known, final, last_arrays, state)

    attn_out = lax.cond(most > 2 * chunk, with_late, without_late, 0)
    new_pages = fresh.reshape(1, half_len // page_len, page_len * lat_width)
    return (attn_out[None], new_pages)


def solution(mesh):
    placed = (
        P(("groups", "req"), "seq", "head"),
        P(("groups", "req"), "seq", "head"),
        P("head", None),
        P(),
        P("head", None, None),
        P("head", None, None),
        P(("groups", "head", "req"), None),
        P("groups", None, None),
        P("groups", None),
        P("groups"),
        P("groups"),
    )
    return jax.shard_map(
        local,
        mesh=mesh,
        in_specs=placed,
        out_specs=(P(("groups", "req"), "seq", "head"), P(("groups", "req"), "seq", None)),
        check_vma=False,
    )
```

profile of v0, /device:TPU:0, one launch (start us, length us, event | category | flops | bytes accessed | tf_op | source)
XLA Modules:
  0.0 123.7 jit_solution(10074370102487314393)
XLA Ops:
  0.6 4.9 %pick_pages.1 = (s32[2]{0:T(128)}, s32[1]{0:T(128)}, bf16[8,32,1152]{2,1,0:T(8,128)(2,1)}, bf16[8,32,1152]{2,1,0:T(8,128)(2,1)}, bf16[1,8,32,1152]{3,2,1,0:T(8,128)(2,1)}, /*index=5*/f32[128,576]{1,0:T(8,128)}) custom-call(s32[2,64]{1,0:T(2,128)} %bitcast.90, s32[2,64]{1,0:T(2,128)} %slot_hbm.1, s32[2]{0:T(128)} %prefix_hbm.1, bf16[32,36864]{1,0:T(8,128)(2,1)} %pool_hbm.1, ...), custom_call_target="tpu_custom_call" | custom-call | flops 1000000000 | bytes 6000000 | tf_op jit(solution)/shard_map/pick_pages/pallas_call | solution.py:158
  5.6 6.3 %all-to-all-start = ((f32[4,32,576]{2,1,0:T(8,128)}), f32[4,32,576]{2,1,0:T(8,128)S(1)}, u32[]{:S(2)}, u32[]{:S(2)}) async-start(f32[4,32,576]{2,1,0:T(8,128)} %bitcast.87), calls=%async_computation | async-start | bytes 655360 | tf_op jit(solution)/shard_map/all_to_all | solution.py:735
  11.9 1.5 %collective-permute-start.6 = (bf16[8,32,1152]{2,1,0:T(8,128)(2,1)}, bf16[8,32,1152]{2,1,0:T(8,128)(2,1)S(1)}, u32[]{:S(2)}, u32[]{:S(2)}) collective-permute-start(bf16[8,32,1152]{2,1,0:T(8,128)(2,1)} %bitcast.91), channel_id=1, source_target_pairs={{0,2},{2,0},{1,3},{3,1},{4,6},{6,4},{5,7},{7,5},{8,10},{10,8},{9,1... | collective-permute-start | bytes 1769480 | tf_op jit(solution)/shard_map/ppermute | solution.py:730
  13.4 4.0 %collective-permute-start.7 = (bf16[8,32,1152]{2,1,0:T(8,128)(2,1)}, bf16[8,32,1152]{2,1,0:T(8,128)(2,1)S(1)}, u32[]{:S(2)}, u32[]{:S(2)}) collective-permute-start(bf16[8,32,1152]{2,1,0:T(8,128)(2,1)} %get-tuple-element.173.refs_0_), channel_id=1, source_target_pairs={{0,4},{5,1},{4,8},{9,5},{8,12},{13,9},{2,6},{7,3},{6,10},{11,7},{1... | collective-permute-start | bytes 1769480 | tf_op jit(solution)/shard_map/ppermute | solution.py:706
  17.4 1.3 %dynamic_slice.12 = s32[1]{0:T(128)} dynamic-slice(s32[2]{0:T(128)} %prefix_hbm.1, s32[]{:T(128)S(6)} %select_n.50), dynamic_slice_sizes={1} | dynamic-slice | bytes 12 | tf_op jit(solution)/shard_map/jit(dynamic_index_in_dim)/dynamic_slice | solution.py:708
  18.7 1.2 dynamic_slice.11.refs_5_
  19.9 0.7 add_convert_fusion.1
  20.6 0.6 fusion.11
  21.2 2.1 %all-to-all-done = f32[4,32,576]{2,1,0:T(8,128)S(1)} async-done(((f32[4,32,576]{2,1,0:T(8,128)}), f32[4,32,576]{2,1,0:T(8,128)S(1)}, u32[]{:S(2)}, u32[]{:S(2)}) %all-to-all-start) | async-done | bytes 294944 | tf_op jit(solution)/shard_map/all_to_all | solution.py:735
  23.3 0.1 multiply_reduce_fusion
  23.4 0.8 multiply_convert_fusion
  24.2 0.1 fusion.5
  24.3 0.1 maximum_select_fusion.1
  24.4 0.7 pad_maximum_fusion
  25.1 3.3 %all-to-all-start.1 = ((bf16[4,32,576]{2,1,0:T(8,128)(2,1)}), bf16[4,32,576]{2,1,0:T(8,128)(2,1)S(1)}, u32[]{:S(2)}, u32[]{:S(2)}) async-start(bf16[4,32,576]{2,1,0:T(8,128)(2,1)} %bitcast.19), calls=%async_computation.1 | async-start | bytes 327680 | tf_op jit(solution)/shard_map/all_to_all | solution.py:740
  28.5 1.6 %collective-permute-start.13 = (s32[1]{0:T(128)}, s32[1]{0:T(128)}, u32[]{:S(2)}, u32[]{:S(2)}) collective-permute-start(s32[1]{0:T(128)} %get-tuple-element.183), channel_id=1, source_target_pairs={{0,16},{16,0},{1,17},{17,1},{2,18},{18,2},{3,19},{19,3},{4,20},{20... | collective-permute-start | bytes 20 | tf_op jit(solution)/shard_map/ppermute | solution.py:257
  30.0 4.4 %all-to-all-done.1 = bf16[4,32,576]{2,1,0:T(8,128)(2,1)S(1)} async-done(((bf16[4,32,576]{2,1,0:T(8,128)(2,1)}), bf16[4,32,576]{2,1,0:T(8,128)(2,1)S(1)}, u32[]{:S(2)}, u32[]{:S(2)}) %all-to-all-start.1) | async-done | bytes 147488 | tf_op jit(solution)/shard_map/all_to_all | solution.py:740
  34.5 0.7 copy-done.12
  35.1 4.2 %collective-permute-start.9 = (bf16[8,32,1152]{2,1,0:T(8,128)(2,1)S(1)}, bf16[8,32,1152]{2,1,0:T(8,128)(2,1)}, u32[]{:S(2)}, u32[]{:S(2)}) collective-permute-start(bf16[8,32,1152]{2,1,0:T(8,128)(2,1)S(1)} %collective-permute-done.7.refs_1_), channel_id=1, source_target_pairs={{0,4},{5,1},{4,8},{9,5},{8,12},{13,9},{2,6},{7,3},{6,10},{11,7},{1... | collective-permute-start | bytes 1769480 | tf_op jit(solution)/shard_map/ppermute | solution.py:706
  39.3 0.7 iota_add_fusion
  39.9 0.7 and_select_fusion.1
  40.6 0.7 fusion.10
  41.3 0.2 convert_reduce_fusion
  41.5 1.1 copy-done.2
  42.6 0.7 copy-done.6
  43.2 4.3 %join_pages.1 = (bf16[16,32,1152]{2,1,0:T(8,128)(2,1)S(1)}, bf16[8,32,1152]{2,1,0:T(8,128)(2,1)}) custom-call(s32[2]{0:T(128)S(1)} %copy-done.6, bf16[8,32,1152]{2,1,0:T(8,128)(2,1)S(1)} %copy-done.2, bf16[1,8,32,1152]{3,2,1,0:T(8,128)(2,1)S(1)} %bitcast.80, bf16[1,8,32,1152]{3,2,1,0:T(8,128)(2,1)S(1)} %collective-permute-done.8.other_ref), custom_call_target="tpu_custom_call" | custom-call | bytes 3000000 | tf_op jit(solution)/shard_map/join_pages/pallas_call | solution.py:223
  47.6 2.8 %collective-permute-start.10 = (bf16[16,32,1152]{2,1,0:T(8,128)(2,1)S(1)}, bf16[16,32,1152]{2,1,0:T(8,128)(2,1)S(1)}, u32[]{:S(2)}, u32[]{:S(2)}) collective-permute-start(bf16[16,32,1152]{2,1,0:T(8,128)(2,1)S(1)} %get-tuple-element.179.refs_7_), channel_id=1, source_target_pairs={{0,4},{5,1},{4,8},{9,5},{8,12},{13,9},{2,6},{7,3},{6,10},{11,7},{1... | collective-permute-start | bytes 3538952 | tf_op jit(solution)/shard_map/ppermute | solution.py:706
  50.4 0.7 subtract_clamp_fusion
  51.1 0.1 select_reduce_fusion
  51.2 0.1 broadcast_in_dim.80
  51.3 0.1 stack.31
  51.4 0.1 iota_compare_fusion.1
  51.5 0.5 collective-permute-start.12
  52.0 0.1 select_reduce_fusion.1
  52.7 0.6 slice_bitcast_fusion.16
  53.3 0.7 concatenate.47.limit_ref
  54.1 0.7 multiply_sine_fusion
  54.9 1.2 copy-done
  56.1 1.0 copy-done.3
  57.1 0.8 turn_queries.1.queries_ref
  59.1 2.8 %collective-permute-start.14 = (bf16[8,32,1152]{2,1,0:T(8,128)(2,1)}, bf16[8,32,1152]{2,1,0:T(8,128)(2,1)}, u32[]{:S(2)}, u32[]{:S(2)}) collective-permute-start(bf16[8,32,1152]{2,1,0:T(8,128)(2,1)} %collective-permute-done.9.refs_3_), channel_id=1, source_target_pairs={{0,4},{5,1},{4,8},{9,5},{8,12},{13,9},{2,6},{7,3},{6,10},{11,7},{1... | collective-permute-start | bytes 1769480 | tf_op jit(solution)/shard_map/ppermute | solution.py:706
  61.9 1.1 copy-done.1
  63.0 6.6 %score_part.9 = (f32[26,512,1024]{2,1,0:T(8,128)}, bf16[26,512,512]{2,1,0:T(8,128)(2,1)}, f32[26,1024]{1,0:T(8,128)S(1)}, f32[1,1024]{1,0:T(1,128)S(1)}, f32[1,1024]{1,0:T(1,128)S(1)}) custom-call(s32[40]{0:T(128)S(1)} %concatenate.47.limit_ref, bf16[640,1024]{1,0:T(8,128)(2,1)S(1)} %turn_queries.1.queries_ref, bf16[8,32,1152]{2,1,0:T(8,128)(2,1)S(1)} %copy-done.1, ...), custom_call_target="tpu_custom_call" | custom-call | flops 1310720 | bytes 100000 | tf_op jit(solution)/shard_map/score_part/pallas_call | solution.py:487
  69.6 0.6 copy-done.4
  70.2 4.2 %collective-permute-start.17 = (bf16[16,32,1152]{2,1,0:T(8,128)(2,1)S(1)}, bf16[16,32,1152]{2,1,0:T(8,128)(2,1)S(1)}, u32[]{:S(2)}, u32[]{:S(2)}) collective-permute-start(bf16[16,32,1152]{2,1,0:T(8,128)(2,1)S(1)} %collective-permute-done.10.refs_8_), channel_id=1, source_target_pairs={{0,4},{5,1},{4,8},{9,5},{8,12},{13,9},{2,6},{7,3},{6,10},{11,7},{1... | collective-permute-start | bytes 3538952 | tf_op jit(solution)/shard_map/ppermute | solution.py:706
  74.5 0.1 collective-permute-start.15
  74.6 0.5 collective-permute-start.18
  75.1 0.7 slice_bitcast_fusion.10
  75.7 1.3 %concatenate.51.limit_ref = s32[64]{0:T(128)} concatenate(s32[8]{0:T(128)} %get-tuple-element.238, s32[8]{0:T(128)} %get-tuple-element.237, s32[16]{0:T(128)} %get-tuple-element.236, s32[16]{0:T(128)} %get-tuple-element.235, s32[16]{0:T(128)} %get-tuple-element.234), dimensions={0} | concatenate | bytes 512 | tf_op jit(solution)/shard_map/concatenate | solution.py:757
  77.1 1.2 %maximum_select_fusion.refs_6_ = bf16[256,576]{1,0:T(8,128)(2,1)S(1)} fusion(bf16[128,576]{1,0:T(8,128)(2,1)} %collective-permute-done.18, bf16[128,576]{1,0:T(8,128)(2,1)} %bitcast.84, pred[]{:T(512)S(6)} %eq.70), kind=kLoop, calls=%fused_computation.13 | loop fusion | flops 1327104 | bytes 589825 | tf_op jit(solution)/shard_map/jit(_where)/select_n | solution.py:818
  78.4 0.9 copy-done.5
  79.3 9.7 %score_part.10 = (f32[26,512,1024]{2,1,0:T(8,128)}, bf16[26,512,512]{2,1,0:T(8,128)(2,1)}, f32[26,1024]{1,0:T(8,128)S(1)}, f32[1,1024]{1,0:T(1,128)S(1)}, f32[1,1024]{1,0:T(1,128)S(1)}) custom-call(s32[64]{0:T(128)} %concatenate.51.limit_ref, bf16[640,1024]{1,0:T(8,128)(2,1)} %copy-done.7, ...), custom_call_target="tpu_custom_call", output_to_operand_aliasing={{0}: (5, {}), {1}: (6, {})} | custom-call | flops 2097152 | bytes 100000 | tf_op jit(solution)/shard_map/score_part/pallas_call | solution.py:487
  89.2 4.4 %collective-permute-start.20 = (bf16[16,32,1152]{2,1,0:T(8,128)(2,1)S(1)}, bf16[16,32,1152]{2,1,0:T(8,128)(2,1)}, u32[]{:S(2)}, u32[]{:S(2)}) collective-permute-start(bf16[16,32,1152]{2,1,0:T(8,128)(2,1)S(1)} %collective-permute-done.17.refs_7_), channel_id=1, source_target_pairs={{0,4},{5,1},{4,8},{9,5},{8,12},{13,9},{2,6},{7,3},{6,10},{11,7},{1... | collective-permute-start | bytes 3538952 | tf_op jit(solution)/shard_map/ppermute | solution.py:706
  93.5 0.1 pad_add_fusion.5.limit_ref
  93.8 7.0 %score_part.11 = (f32[26,512,1024]{2,1,0:T(8,128)}, bf16[26,512,512]{2,1,0:T(8,128)(2,1)}, f32[26,1024]{1,0:T(8,128)S(1)}, f32[1,1024]{1,0:T(1,128)S(1)}, f32[1,...) custom-call(s32[32]{0:T(128)S(1)} %pad_add_fusion.5.limit_ref, ...), custom_call_target="tpu_custom_call", output_to_operand_aliasing={{0}: (5, {}), {1}: (6, {})} | custom-call | flops 1048576 | bytes 100000 | tf_op jit(solution)/shard_map/score_part/pallas_call | solution.py:487
  100.8 5.4 %collective-permute-done.20 = bf16[16,32,1152]{2,1,0:T(8,128)(2,1)} collective-permute-done((bf16[16,32,1152]{2,1,0:T(8,128)(2,1)S(1)}, bf16[16,32,1152]{2,1,0:T(8,128)(2,1)}, u32[]{:S(2)}, u32[]{:S(2)}) %collective-permute-start.20) | collective-permute-done | bytes 1179680 | tf_op jit(solution)/shard_map/ppermute | solution.py:706
  106.2 0.5 collective-permute-start.21
  106.8 0.1 concatenate.48
  106.9 0.1 pad_add_fusion.4
  107.0 0.9 reshape.204
  107.9 1.5 %collective-permute-done.21 = bf16[16,32,1152]{2,1,0:T(8,128)(2,1)S(1)} collective-permute-done((bf16[16,32,1152]{2,1,0:T(8,128)(2,1)}, bf16[16,32,1152]{2,1,0:T(8,128)(2,1)S(1)}, u32[]{:S(2)}, u32[]{:S(2)}) %collective-permute-start.21) | collective-permute-done | bytes 1179680 | tf_op jit(solution)/shard_map/ppermute | solution.py:703
  109.4 13.6 %conditional.1 = (bf16[1,128,1024]{2,1,0:T(8,128)(2,1)S(1)}) conditional(s32[]{:T(128)} %convert_element_type.28, (s32[136]{0:T(256)S(1)}, s32[32]{0:T(128)S(1)}, bf16[640,1024]{1,0:T(8,128)(2,1)S(1)}, f32[26,1024]{1,0:T(8,128)S(1)}, f32[1,1024]{1,0:T(1,128)S(1)}, /*index=5*/f32[1,1024]{1,0:T(1,128)S(1)}, f32[256,1024]{1,0:T(8,128)}, ...), branch_computations={%region_6.7_spmd, %region_7.8_spmd} | conditional | flops 8055422976 | bytes 57044920 | solution.py:867
  109.4 13.3 %finish.2 = bf16[128,1024]{1,0:T(8,128)(2,1)S(1)} custom-call(s32[136]{0:T(256)S(1)} %get-tuple-element.70.limit_ref, s32[32]{0:T(128)S(1)} %get-tuple-element.71.last_limit_ref, bf16[640,1024]{1,0:T(8,128)(2,1)S(1)} %get-tuple-element.72.queries_ref, f32[26,1024]{1,0:T(8,128)S(1)} %get-tuple-element.73.marks, f32[1,1024]{1,0:T(1,128)S(1)} %get-tuple-element.74.sum_in, ...), custom_call_target="tpu_custom_call" | custom-call | flops 6442450944 | bytes 30000000 | tf_op jit(solution)/shard_map/cond/branch_0_fun/finish/pallas_call | solution.py:623
  123.0 0.7 copy-done.16
  (80 shorter events, 0.4 us)
Async XLA Ops:
  5.6 17.7 %all-to-all-start = ((f32[4,32,576]{2,1,0:T(8,128)}), f32[4,32,576]{2,1,0:T(8,128)S(1)}, u32[]{:S(2)}, u32[]{:S(2)}) async-start(f32[4,32,576]{2,1,0:T(8,128)} %bitcast.87), calls=%async_computation | async-start | bytes 655360 | tf_op jit(solution)/shard_map/all_to_all | solution.py:735
  11.9 22.5 %collective-permute-start.6 = (bf16[8,32,1152]{2,1,0:T(8,128)(2,1)}, bf16[8,32,1152]{2,1,0:T(8,128)(2,1)S(1)}, u32[]{:S(2)}, u32[]{:S(2)}) collective-permute-start(bf16[8,32,1152]{2,1,0:T(8,128)(2,1)} %bitcast.91), channel_id=1, source_target_pairs={{0,2},{2,0},{1,3},{3,1},{4,6},{6,4},{5,7},{7,5},{8,10},{10,8},{9,1... | collective-permute-start | bytes 1769480 | tf_op jit(solution)/shard_map/ppermute | solution.py:730
  13.4 16.6 %collective-permute-start.7 = (bf16[8,32,1152]{2,1,0:T(8,128)(2,1)}, bf16[8,32,1152]{2,1,0:T(8,128)(2,1)S(1)}, u32[]{:S(2)}, u32[]{:S(2)}) collective-permute-start(bf16[8,32,1152]{2,1,0:T(8,128)(2,1)} %get-tuple-element.173.refs_0_), channel_id=1, source_target_pairs={{0,4},{5,1},{4,8},{9,5},{8,12},{13,9},{2,6},{7,3},{6,10},{11,7},{1... | collective-permute-start | bytes 1769480 | tf_op jit(solution)/shard_map/ppermute | solution.py:706
  19.9 14.6 %copy-start.32 = (f32[32]{0:T(128)}, f32[32]{0:T(128)S(1)}, u32[]{:S(2)}) copy-start(f32[32]{0:T(128)S(1)} %multiply_power_fusion) | copy-start | bytes 388
  25.1 9.3 %all-to-all-start.1 = ((bf16[4,32,576]{2,1,0:T(8,128)(2,1)}), bf16[4,32,576]{2,1,0:T(8,128)(2,1)S(1)}, u32[]{:S(2)}, u32[]{:S(2)}) async-start(bf16[4,32,576]{2,1,0:T(8,128)(2,1)} %bitcast.19), calls=%async_computation.1 | async-start | bytes 327680 | tf_op jit(solution)/shard_map/all_to_all | solution.py:740
  28.5 29.4 %collective-permute-start.13 = (s32[1]{0:T(128)}, s32[1]{0:T(128)}, u32[]{:S(2)}, u32[]{:S(2)}) collective-permute-start(s32[1]{0:T(128)} %get-tuple-element.183), channel_id=1, source_target_pairs={{0,16},{16,0},{1,17},{17,1},{2,18},{18,2},{3,19},{19,3},{4,20},{20... | collective-permute-start | bytes 20 | tf_op jit(solution)/shard_map/ppermute | solution.py:257
  34.4 0.7 copy-start.12
  35.1 6.4 %collective-permute-start.8 = (bf16[1,8,32,1152]{3,2,1,0:T(8,128)(2,1)S(1)}, bf16[1,8,32,1152]{3,2,1,0:T(8,128)(2,1)S(1)}, u32[]{:S(2)}, u32[]{:S(2)}) collective-permute-start(bf16[1,8,32,1152]{3,2,1,0:T(8,128)(2,1)S(1)} %bitcast.79), channel_id=1, source_target_pairs={{0,1},{1,0},{2,3},{3,2},{4,5},{5,4},{6,7},{7,6},{8,9},{9,8},{10,11... | collective-permute-start | bytes 1769480 | tf_op jit(solution)/shard_map/ppermute | solution.py:703
  35.1 12.4 %collective-permute-start.9 = (bf16[8,32,1152]{2,1,0:T(8,128)(2,1)S(1)}, bf16[8,32,1152]{2,1,0:T(8,128)(2,1)}, u32[]{:S(2)}, u32[]{:S(2)}) collective-permute-start(bf16[8,32,1152]{2,1,0:T(8,128)(2,1)S(1)} %collective-permute-done.7.refs_1_), channel_id=1, source_target_pairs={{0,4},{5,1},{4,8},{9,5},{8,12},{13,9},{2,6},{7,3},{6,10},{11,7},{1... | collective-permute-start | bytes 1769480 | tf_op jit(solution)/shard_map/ppermute | solution.py:706
  41.5 1.1 copy-start.2
  42.6 0.7 copy-start.6
  47.6 22.7 %collective-permute-start.10 = (bf16[16,32,1152]{2,1,0:T(8,128)(2,1)S(1)}, bf16[16,32,1152]{2,1,0:T(8,128)(2,1)S(1)}, u32[]{:S(2)}, u32[]{:S(2)}) collective-permute-start(bf16[16,32,1152]{2,1,0:T(8,128)(2,1)S(1)} %get-tuple-element.179.refs_7_), channel_id=1, source_target_pairs={{0,4},{5,1},{4,8},{9,5},{8,12},{13,9},{2,6},{7,3},{6,10},{11,7},{1... | collective-permute-start | bytes 3538952 | tf_op jit(solution)/shard_map/ppermute | solution.py:706
  51.5 10.4 %collective-permute-start.11 = (bf16[8,32,1152]{2,1,0:T(8,128)(2,1)S(1)}, bf16[8,32,1152]{2,1,0:T(8,128)(2,1)S(1)}, u32[]{:S(2)}, u32[]{:S(2)}) collective-permute-start(bf16[8,32,1152]{2,1,0:T(8,128)(2,1)S(1)} %collective-permute-done.7.refs_1_), channel_id=1, source_target_pairs={{0,1},{1,0},{2,3},{3,2},{4,5},{5,4},{6,7},{7,6},{8,9},{9,8},{10,11... | collective-permute-start | bytes 1769480 | tf_op jit(solution)/shard_map/ppermute | solution.py:703
  51.5 10.4 %collective-permute-start.12 = (bf16[8,32,1152]{2,1,0:T(8,128)(2,1)}, bf16[8,32,1152]{2,1,0:T(8,128)(2,1)}, u32[]{:S(2)}, u32[]{:S(2)}) collective-permute-start(bf16[8,32,1152]{2,1,0:T(8,128)(2,1)} %collective-permute-done.9.refs_3_), channel_id=1, source_target_pairs={{0,1},{1,0},{2,3},{3,2},{4,5},{5,4},{6,7},{7,6},{8,9},{9,8},{10,11... | collective-permute-start | bytes 1769480 | tf_op jit(solution)/shard_map/ppermute | solution.py:703
  53.3 8.6 %copy-start.21 = (s32[8]{0:T(128)}, s32[8]{0:T(128)S(1)}, u32[]{:S(2)}) copy-start(s32[8]{0:T(128)S(1)} %get-tuple-element.239) | copy-start | bytes 100
  53.3 8.6 %copy-start.23 = (s32[8]{0:T(128)}, s32[8]{0:T(128)S(1)}, u32[]{:S(2)}) copy-start(s32[8]{0:T(128)S(1)} %get-tuple-element.240) | copy-start | bytes 100
  54.1 35.0 %copy-start.17 = (s32[40]{0:T(128)}, s32[40]{0:T(128)S(1)}, u32[]{:S(2)}) copy-start(s32[40]{0:T(128)S(1)} %concatenate.47.limit_ref) | copy-start | bytes 484
  54.8 1.2 copy-start
  56.1 1.0 copy-start.3
  57.9 12.4 %copy-start.7 = (bf16[640,1024]{1,0:T(8,128)(2,1)}, bf16[640,1024]{1,0:T(8,128)(2,1)S(1)}, u32[]{:S(2)}) copy-start(bf16[640,1024]{1,0:T(8,128)(2,1)S(1)} %turn_queries.1.queries_ref) | copy-start | bytes 3932164
  59.1 15.4 %collective-permute-start.14 = (bf16[8,32,1152]{2,1,0:T(8,128)(2,1)}, bf16[8,32,1152]{2,1,0:T(8,128)(2,1)}, u32[]{:S(2)}, u32[]{:S(2)}) collective-permute-start(bf16[8,32,1152]{2,1,0:T(8,128)(2,1)} %collective-permute-done.9.refs_3_), channel_id=1, source_target_pairs={{0,4},{5,1},{4,8},{9,5},{8,12},{13,9},{2,6},{7,3},{6,10},{11,7},{1... | collective-permute-start | bytes 1769480 | tf_op jit(solution)/shard_map/ppermute | solution.py:706
  61.9 1.1 copy-start.1
  69.6 0.7 copy-start.4
  70.2 8.2 %collective-permute-start.16 = (bf16[16,32,1152]{2,1,0:T(8,128)(2,1)S(1)}, bf16[16,32,1152]{2,1,0:T(8,128)(2,1)}, u32[]{:S(2)}, u32[]{:S(2)}) collective-permute-start(bf16[16,32,1152]{2,1,0:T(8,128)(2,1)S(1)} %collective-permute-done.10.refs_8_), channel_id=1, source_target_pairs={{0,1},{1,0},{2,3},{3,2},{4,5},{5,4},{6,7},{7,6},{8,9},{9,8},{10,11... | collective-permute-start | bytes 3538952 | tf_op jit(solution)/shard_map/ppermute | solution.py:703
  70.2 18.9 %collective-permute-start.17 = (bf16[16,32,1152]{2,1,0:T(8,128)(2,1)S(1)}, bf16[16,32,1152]{2,1,0:T(8,128)(2,1)S(1)}, u32[]{:S(2)}, u32[]{:S(2)}) collective-permute-start(bf16[16,32,1152]{2,1,0:T(8,128)(2,1)S(1)} %collective-permute-done.10.refs_8_), channel_id=1, source_target_pairs={{0,4},{5,1},{4,8},{9,5},{8,12},{13,9},{2,6},{7,3},{6,10},{11,7},{1... | collective-permute-start | bytes 3538952 | tf_op jit(solution)/shard_map/ppermute | solution.py:706
  74.5 3.9 %collective-permute-start.15 = (bf16[8,32,1152]{2,1,0:T(8,128)(2,1)}, bf16[8,32,1152]{2,1,0:T(8,128)(2,1)}, u32[]{:S(2)}, u32[]{:S(2)}) collective-permute-start(bf16[8,32,1152]{2,1,0:T(8,128)(2,1)} %collective-permute-done.14.refs_5_), channel_id=1, source_target_pairs={{0,1},{1,0},{2,3},{3,2},{4,5},{5,4},{6,7},{7,6},{8,9},{9,8},{10,11... | collective-permute-start | bytes 1769480 | tf_op jit(solution)/shard_map/ppermute | solution.py:703
  74.6 2.6 %collective-permute-start.18 = (bf16[128,576]{1,0:T(8,128)(2,1)}, bf16[128,576]{1,0:T(8,128)(2,1)}, u32[]{:S(2)}, u32[]{:S(2)}) collective-permute-start(bf16[128,576]{1,0:T(8,128)(2,1)} %bitcast.83), channel_id=1, source_target_pairs={{0,1},{1,0},{2,3},{3,2},{4,5},{5,4},{6,7},{7,6},{8,9},{9,8},{10,11... | collective-permute-start | bytes 442376 | tf_op jit(solution)/shard_map/ppermute | solution.py:703
  78.4 0.9 copy-start.5
  79.3 14.2 %copy-start.33 = (s32[16]{0:T(128)S(1)}, s32[16]{0:T(128)}, u32[]{:S(2)}) copy-start(s32[16]{0:T(128)} %get-tuple-element.232) | copy-start | bytes 196
  79.3 14.2 %copy-start.35 = (s32[16]{0:T(128)S(1)}, s32[16]{0:T(128)}, u32[]{:S(2)}) copy-start(s32[16]{0:T(128)} %get-tuple-element.233) | copy-start | bytes 196
  79.3 14.3 %copy-start.8 = (bf16[640,1024]{1,0:T(8,128)(2,1)S(1)}, bf16[640,1024]{1,0:T(8,128)(2,1)}, u32[]{:S(2)}) copy-start(bf16[640,1024]{1,0:T(8,128)(2,1)} %copy-done.7) | copy-start | bytes 3932164
  89.1 4.5 %collective-permute-start.19 = (bf16[16,32,1152]{2,1,0:T(8,128)(2,1)S(1)}, bf16[16,32,1152]{2,1,0:T(8,128)(2,1)S(1)}, u32[]{:S(2)}, u32[]{:S(2)}) collective-permute-start(bf16[16,32,1152]{2,1,0:T(8,128)(2,1)S(1)} %collective-permute-done.17.refs_7_), channel_id=1, source_target_pairs={{0,1},{1,0},{2,3},{3,2},{4,5},{5,4},{6,7},{7,6},{8,9},{9,8},{10,11... | collective-permute-start | bytes 3538952 | tf_op jit(solution)/shard_map/ppermute | solution.py:703
  89.2 17.0 %collective-permute-start.20 = (bf16[16,32,1152]{2,1,0:T(8,128)(2,1)S(1)}, bf16[16,32,1152]{2,1,0:T(8,128)(2,1)}, u32[]{:S(2)}, u32[]{:S(2)}) collective-permute-start(bf16[16,32,1152]{2,1,0:T(8,128)(2,1)S(1)} %collective-permute-done.17.refs_7_), channel_id=1, source_target_pairs={{0,4},{5,1},{4,8},{9,5},{8,12},{13,9},{2,6},{7,3},{6,10},{11,7},{1... | collective-permute-start | bytes 3538952 | tf_op jit(solution)/shard_map/ppermute | solution.py:706
  93.6 13.1 %copy-start.19 = (s32[8]{0:T(128)S(1)}, s32[8]{0:T(128)}, u32[]{:S(2)}) copy-start(s32[8]{0:T(128)} %get-tuple-element.237) | copy-start | bytes 100
  93.6 13.1 %copy-start.20 = (s32[8]{0:T(128)S(1)}, s32[8]{0:T(128)}, u32[]{:S(2)}) copy-start(s32[8]{0:T(128)} %get-tuple-element.238) | copy-start | bytes 100
  93.6 13.1 %copy-start.22 = (s32[8]{0:T(128)S(1)}, s32[8]{0:T(128)}, u32[]{:S(2)}) copy-start(s32[8]{0:T(128)} %copy-done.21) | copy-start | bytes 100
  93.6 13.1 %copy-start.24 = (s32[8]{0:T(128)S(1)}, s32[8]{0:T(128)}, u32[]{:S(2)}) copy-start(s32[8]{0:T(128)} %copy-done.23) | copy-start | bytes 100
  93.6 13.1 %copy-start.25 = (s32[8]{0:T(128)S(1)}, s32[8]{0:T(128)}, u32[]{:S(2)}) copy-start(s32[8]{0:T(128)} %get-tuple-element.241) | copy-start | bytes 100
  93.7 13.1 %copy-start.26 = (s32[8]{0:T(128)S(1)}, s32[8]{0:T(128)}, u32[]{:S(2)}) copy-start(s32[8]{0:T(128)} %get-tuple-element.242) | copy-start | bytes 100
  93.7 13.1 %copy-start.27 = (s32[8]{0:T(128)S(1)}, s32[8]{0:T(128)}, u32[]{:S(2)}) copy-start(s32[8]{0:T(128)} %get-tuple-element.243) | copy-start | bytes 100
  93.7 13.1 %copy-start.28 = (s32[16]{0:T(128)S(1)}, s32[16]{0:T(128)}, u32[]{:S(2)}) copy-start(s32[16]{0:T(128)} %get-tuple-element.234) | copy-start | bytes 196
  93.7 13.1 %copy-start.29 = (s32[16]{0:T(128)S(1)}, s32[16]{0:T(128)}, u32[]{:S(2)}) copy-start(s32[16]{0:T(128)} %get-tuple-element.235) | copy-start | bytes 196
  93.7 13.1 %copy-start.30 = (s32[16]{0:T(128)S(1)}, s32[16]{0:T(128)}, u32[]{:S(2)}) copy-start(s32[16]{0:T(128)} %get-tuple-element.236) | copy-start | bytes 196
  93.7 13.1 %copy-start.34 = (s32[16]{0:T(128)S(1)}, s32[16]{0:T(128)}, u32[]{:S(2)}) copy-start(s32[16]{0:T(128)} %get-tuple-element.232) | copy-start | bytes 196
  93.7 13.1 %copy-start.36 = (s32[16]{0:T(128)S(1)}, s32[16]{0:T(128)}, u32[]{:S(2)}) copy-start(s32[16]{0:T(128)} %get-tuple-element.233) | copy-start | bytes 196
  93.7 13.2 %copy-start.39 = (s32[16]{0:T(128)S(1)}, s32[16]{0:T(128)}, u32[]{:S(2)}) copy-start(s32[16]{0:T(128)} %get-tuple-element.230) | copy-start | bytes 196
  93.7 13.2 %copy-start.40 = (s32[16]{0:T(128)S(1)}, s32[16]{0:T(128)}, u32[]{:S(2)}) copy-start(s32[16]{0:T(128)} %get-tuple-element.231) | copy-start | bytes 196
  93.7 13.2 %copy-start.13 = (bf16[4,32,576]{2,1,0:T(8,128)(2,1)S(1)}, bf16[4,32,576]{2,1,0:T(8,128)(2,1)}, u32[]{:S(2)}) copy-start(bf16[4,32,576]{2,1,0:T(8,128)(2,1)} %copy-done.12) | copy-start | bytes 442372
  93.8 15.6 %copy-start.9 = (bf16[640,1024]{1,0:T(8,128)(2,1)S(1)}, bf16[640,1024]{1,0:T(8,128)(2,1)}, u32[]{:S(2)}) copy-start(bf16[640,1024]{1,0:T(8,128)(2,1)} %copy-done.7) | copy-start | bytes 3932164
  106.2 3.2 %collective-permute-start.21 = (bf16[16,32,1152]{2,1,0:T(8,128)(2,1)}, bf16[16,32,1152]{2,1,0:T(8,128)(2,1)S(1)}, u32[]{:S(2)}, u32[]{:S(2)}) collective-permute-start(bf16[16,32,1152]{2,1,0:T(8,128)(2,1)} %collective-permute-done.20), channel_id=1, source_target_pairs={{0,1},{1,0},{2,3},{3,2},{4,5},{5,4},{6,7},{7,6},{8,9},{9,8},{10,11... | collective-permute-start | bytes 3538952 | tf_op jit(solution)/shard_map/ppermute | solution.py:703
  123.0 0.7 copy-start.16
where the time goes:
time: 125 us; the launch traced here: 124 us
  Pallas kernels  46.7 us (37%)
  starting transfers between devices  36.7 us (29%)
  local copies, waits for them, and re-layouts  15 us (12%)
  waiting for transfers between devices  13.6 us (11%)
  other arithmetic  8.35 us (7%)
  between operations  3.1 us (2%)
    pallas_call x3, Pallas kernels, score_part(): pl.pallas_call(functools.partial(score_kernel, shape, base, len(sources),...  23.3 us
    ppermute x6, starting transfers between devices, stream(): return lax.ppermute(block, ('head', 'seq'), stream_route)  22.3 us
    pallas_call x1, Pallas kernels, finish(): pl.pallas_call(functools.partial(finish_kernel, shape, depth, n_blocks, l...  13.3 us
    unnamed x66, local copies, waits for them, and re-layouts  7.99 us
    all_to_all x1, starting transfers between devices, local(): lax.all_to_all(partial_value, 'head', split_axis=0, concat_axis=0, tiled=...  6.33 us
    ppermute x6, waiting for transfers between devices, stream(): return lax.ppermute(block, ('head', 'seq'), stream_route)  5.45 us
    pallas_call x1, Pallas kernels, pick_pages(): pl.pallas_call(functools.partial(pick_kernel, cap, 2 * pairs), out_shape=...  4.94 us
    all_to_all x1, waiting for transfers between devices, local(): lax.all_to_all(copies, 'head', split_axis=0, concat_axis=0, tiled=True)  4.39 us
  transfers between devices with their start and end apart: 18, of which 5 were waited for; matrix products, arithmetic and copies ran while one was open for 12% of the time, Pallas kernels for 23%

commit v1 on v0

--- a/solution.py
+++ b/solution.py
@@ -60,9 +60,9 @@
 
 
 def pick_kernel(
-    cap, page_len, owner_hbm, slot_hbm, prefix_hbm, pool_hbm, hidden_hbm, down_hbm, count_ref, most_ref,
-    first_ref, rest_ref, foreign_ref, partial_ref, owner_ref, slot_ref, prefix_ref, pool_ref, hidden_ref,
-    down_ref, pages, lists, table, sems,
+    cap, page_len, owner_hbm, slot_hbm, prefix_hbm, suffix_hbm, pool_hbm, hidden_hbm, down_hbm, count_ref,
+    most_ref, length_ref, live_ref, first_ref, rest_ref, foreign_ref, partial_ref, owner_ref, slot_ref,
+    prefix_ref, suffix_ref, pool_ref, hidden_ref, down_ref, pages, lists, table, sems,
 ):
     n_req = lax.axis_size("req")
     head_idx = lax.axis_index("head")
@@ -78,12 +78,16 @@
         pltpu.make_async_copy(hidden_hbm, hidden_ref, sems.at[6]),
         pltpu.make_async_copy(down_hbm, down_ref, sems.at[7]),
         pltpu.make_async_copy(prefix_hbm, prefix_ref, sems.at[8]),
+        pltpu.make_async_copy(suffix_hbm, suffix_ref, sems.at[9]),
     ]
     for load in loads:
         load.start()
     loads[0].wait()
     loads[1].wait()
     loads[5].wait()
+    loads[6].wait()
+    length_ref[0] = prefix_ref[req_idx]
+    live_ref[0] = suffix_ref[req_idx]
     self_owner = head_idx * n_req + req_idx
     n_owners = table.shape[1]
     for shift in range(n_req):
@@ -151,7 +155,8 @@
 
 
 def pick_pages(
-    page_owner, page_slot, prefix_len, page_pool, hidden, down, cap, chunk, n_head, n_req, n_seq, pairs
+    page_owner, page_slot, prefix_len, suffix_len, page_pool, hidden, down,
+    cap, chunk, n_head, n_req, n_seq, pairs,
 ):
     pool_pages, page_width = page_pool.shape
     page = (pairs, page_width // pairs)
@@ -160,29 +165,32 @@
         out_shape=(
             jax.ShapeDtypeStruct((n_req,), jnp.int32),
             jax.ShapeDtypeStruct((1,), jnp.int32),
+            jax.ShapeDtypeStruct((1,), jnp.int32),
+            jax.ShapeDtypeStruct((1,), jnp.int32),
             jax.ShapeDtypeStruct((chunk, *page), jnp.bfloat16),
             jax.ShapeDtypeStruct((max(1, cap - chunk), *page), jnp.bfloat16),
             jax.ShapeDtypeStruct((n_req - 1, cap // n_seq, *page), jnp.bfloat16),
             jax.ShapeDtypeStruct((hidden.shape[0], down.shape[0]), jnp.float32),
         ),
-        in_specs=[any_spec(), any_spec(), any_spec(), hbm_spec(), hbm_spec(), hbm_spec()],
-        out_specs=(smem_spec(), smem_spec(), hbm_spec(), hbm_spec(), hbm_spec(), vmem_spec()),
+        in_specs=[any_spec()] * 4 + [hbm_spec()] * 3,
+        out_specs=(smem_spec(), smem_spec(), smem_spec(), smem_spec(), hbm_spec(), hbm_spec(), hbm_spec(), vmem_spec()),
         scratch_shapes=[
             pltpu.SMEM(page_owner.shape, jnp.int32),
             pltpu.SMEM(page_slot.shape, jnp.int32),
             pltpu.SMEM(prefix_len.shape, jnp.int32),
+            pltpu.SMEM(suffix_len.shape, jnp.int32),
             pltpu.VMEM((pool_pages, page_width), jnp.bfloat16),
             pltpu.VMEM(hidden.shape, jnp.bfloat16),
             pltpu.VMEM(down.shape, jnp.bfloat16),
             pltpu.VMEM((pool_pages, *page), jnp.bfloat16),
             pltpu.SMEM((n_req, cap + 1), jnp.int32),
             pltpu.SMEM((n_req, n_head * n_req), jnp.int32),
-            pltpu.SemaphoreType.DMA((9,)),
+            pltpu.SemaphoreType.DMA((10,)),
         ],
         compiler_params=pltpu.CompilerParams(vmem_limit_bytes=60 * MIB),
         cost_estimate=pl.CostEstimate(flops=10**9, bytes_accessed=6 * 10**6, transcendentals=0),
         name="pick_pages",
-    )(page_owner, page_slot, prefix_len, page_pool, hidden, down)
+    )(page_owner, page_slot, prefix_len, suffix_len, page_pool, hidden, down)
 
 
 def join_kernel(chunk, cap, count_ref, rest_ref, mine_ref, other_ref, *refs):
@@ -232,22 +240,69 @@
     )(counts, rest, mine, other)
 
 
-def token_limits(owners, prefix, req_idx, n_head, n_req, chunk, slots, page_len):
-    pages = owners.shape[0]
-    order = jnp.arange(pages, dtype=jnp.int32)
-    place = owners // n_req
-    shift = lax.rem(req_idx + n_req - lax.rem(owners, n_req), n_req)
-    key = shift * pages + order
-    together = (place[None, :] == place[:, None]) & (order * page_len < prefix)[None, :]
-    rank = jnp.sum((together & (key[None, :] < key[:, None])).astype(jnp.int32), axis=1)
-    held = jnp.sum((together & (shift[None, :] == 0)).astype(jnp.int32), axis=1)
-    early = (shift == 0) & (rank < chunk)
-    within = jnp.where(early, rank, chunk + rank - jnp.minimum(held, chunk))
-    slot = place * slots + within
-    tokens = jnp.clip(prefix - order * page_len, 0, page_len)
-    all_slots = jnp.arange(n_head * slots, dtype=jnp.int32)
-    limits = jnp.sum(jnp.where(slot[None, :] == all_slots[:, None], tokens[None, :], 0), axis=1)
-    return limits.reshape(n_head, slots)
+def plan_kernel(pieces, page_len, chunk, owner_ref, prefix_ref, limit_ref, places, counts, running):
+    n_req = lax.axis_size("req")
+    head_idx = lax.axis_index("head")
+    req_idx = lax.axis_index("req")
+    n_head, width = places.shape
+    n_pages = owner_ref.shape[1]
+    prefix = prefix_ref[req_idx]
+    for place in range(n_head):
+        for shift in range(n_req):
+            counts[place, shift] = 0
+            running[place, shift] = 0
+        for slot in range(width):
+            places[place, slot] = 0
+
+    def where_from(page):
+        owner = owner_ref[req_idx, page]
+        place = owner // n_req
+        shift = lax.rem(req_idx + n_req - (owner - place * n_req), n_req)
+        return place, shift, (page * page_len < prefix).astype(jnp.int32)
+
+    def count(page, carry):
+        place, shift, needed = where_from(page)
+        counts[place, shift] += needed
+        return carry
+
+    def note(page, carry):
+        place, shift, needed = where_from(page)
+        rank = running[place, shift]
+        running[place, shift] = rank + needed
+        for earlier in range(n_req - 1):
+            rank = rank + jnp.where(earlier < shift, counts[place, earlier], 0)
+        early = (shift == 0) & (rank < chunk)
+        slot = jnp.where(early, rank, chunk + rank - jnp.minimum(counts[place, 0], chunk))
+        slot = jnp.where(needed > 0, slot, width - 1)
+        places[place, slot] = jnp.clip(prefix - page * page_len, 0, page_len)
+        return carry
+
+    lax.fori_loop(0, n_pages, count, 0, unroll=4)
+    lax.fori_loop(0, n_pages, note, 0, unroll=4)
+    upward = 2 * lax.axis_index("seq") - 1
+    for block, (first, origin) in enumerate(pieces):
+        step, side = (origin + 1) // 2, 2 * (origin % 2) - 1
+        place = head_idx + upward * side * step
+        inside = (place >= 0) & (place < n_head)
+        place = jnp.clip(place, 0, n_head - 1)
+        for j in range(chunk):
+            limit_ref[block * chunk + j] = jnp.where(inside, places[place, first + j], 0)
+
+
+def plan_blocks(page_owner, prefix_len, pieces, n_head, n_req, chunk, page_len):
+    return pl.pallas_call(
+        functools.partial(plan_kernel, pieces, page_len, chunk),
+        out_shape=jax.ShapeDtypeStruct((len(pieces) * chunk,), jnp.int32),
+        in_specs=[smem_spec()] * 2,
+        out_specs=smem_spec(),
+        scratch_shapes=[
+            pltpu.SMEM((n_head, 4 * chunk + 1), jnp.int32),
+            pltpu.SMEM((n_head, n_req), jnp.int32),
+            pltpu.SMEM((n_head, n_req), jnp.int32),
+        ],
+        cost_estimate=pl.CostEstimate(flops=10**4, bytes_accessed=10**4, transcendentals=0),
+        name="plan_blocks",
+    )(page_owner, prefix_len)
 
 
 def over_groups(most):
@@ -396,9 +451,9 @@
     def one_block(block, carry):
         pltpu.make_async_copy(blocks.at[block], blocks.at[block], load_sems.at[block]).wait()
 
-        @pl.when(any_token(limit_ref, block, chunk))
+        @pl.when(any_token(limit_ref, base + block, chunk))
         def _():
-            load_block(blocks.at[block], keys, block_limits(limit_ref, block, chunk), key_width)
+            load_block(blocks.at[block], keys, block_limits(limit_ref, base + block, chunk), key_width)
 
             def note(part, new):
                 marks[pl.ds(base + block, 1), part] = new
@@ -429,7 +484,7 @@
         near_values[...] = turn_values(near_keys, latent_width)
 
     def one_wait(block, carry):
-        @pl.when(any_token(limit_ref, block, chunk))
+        @pl.when(any_token(limit_ref, base + block, chunk))
         def _():
             for copy in stores(block):
                 copy.wait()
@@ -500,7 +555,7 @@
 
 
 def finish_kernel(
-    shape, depth, n_blocks, n_sources, limit_ref, last_limit_ref, queries_ref, marks, sum_in, high_in,
+    shape, depth, n_blocks, n_sources, limit_ref, queries_ref, marks, sum_in, high_in,
     near_weights, near_values, near_mark, live_ref, up_ref, weights_hbm, values_hbm, *refs,
 ):
     tile, scale, chunk, key_width = shape
@@ -548,9 +603,9 @@
     def one_score(block, carry):
         pltpu.make_async_copy(blocks.at[block], blocks.at[block], load_sems.at[block]).wait()
 
-        @pl.when(any_token(last_limit_ref, block, chunk))
+        @pl.when(any_token(limit_ref, n_blocks + block, chunk))
         def _():
-            load_block(blocks.at[block], keys, block_limits(last_limit_ref, block, chunk), key_width)
+            load_block(blocks.at[block], keys, block_limits(limit_ref, n_blocks + block, chunk), key_width)
 
             def note(part, new):
                 last_marks[pl.ds(block, 1), part] = new
@@ -588,7 +643,7 @@
     lax.fori_loop(0, n_used, one_add, 0)
 
     def one_last(block, carry):
-        @pl.when(any_token(last_limit_ref, block, chunk))
+        @pl.when(any_token(limit_ref, n_blocks + block, chunk))
         def _():
             add_block(last_weights.at[block], last_values.at[block], last_marks.at[pl.ds(block, 1)])
 
@@ -609,7 +664,7 @@
         ).astype(jnp.bfloat16)
 
 
-def finish(n_blocks, limits, last_limits, queries, state, near_state, sources, live, up_weight, half_len, shape):
+def finish(n_blocks, limits, queries, state, near_state, sources, live, up_weight, half_len, shape):
     tile, scale, chunk, key_width = shape
     weights, values, marks, weight_sum, highest = state
     width, rows = queries.shape
@@ -623,7 +678,7 @@
     return pl.pallas_call(
         functools.partial(finish_kernel, shape, depth, n_blocks, len(sources)),
         out_shape=jax.ShapeDtypeStruct((half_len, heads * value_width), jnp.bfloat16),
-        in_specs=[smem_spec()] * 2
+        in_specs=[smem_spec()]
         + [vmem_spec()] * 7
         + [smem_spec(), vmem_spec()]
         + [hbm_spec()] * (2 + len(sources)),
@@ -650,7 +705,7 @@
         ),
         name="finish",
     )(
-        limits, last_limits, queries, marks, weight_sum, highest, *near_state, live, up_weight,
+        limits, queries, marks, weight_sum, highest, *near_state, live, up_weight,
         weights, values, *sources,
     )
 
@@ -685,12 +740,11 @@
     pages_req = page_slot.shape[1]
     cap = max(2, 2 * pages_req // (n_head * n_req))
     chunk = n_req * cap // 4
-    slots = 4 * chunk
     score_scale = float(query_width) ** (-0.5)
 
     owner_rows = page_owner[:, :, 0]
-    counts, most, first, rest, foreign, partial_value = pick_pages(
-        owner_rows, page_slot, prefix_len, page_pool, hidden[0], w_dkv.T,
+    counts, most, my_prefix, live, first, rest, foreign, partial_value = pick_pages(
+        owner_rows, page_slot, prefix_len, suffix_len, page_pool, hidden[0], w_dkv.T,
         cap, chunk, n_head, n_req, n_seq, pairs,
     )
     swap_route = [(i, n_seq - 1 - i) for i in range(n_seq)]
@@ -705,20 +759,6 @@
     def stream(block):
         return lax.ppermute(block, ("head", "seq"), stream_route)
 
-    my_prefix = lax.dynamic_index_in_dim(prefix_len, req_idx, 0, keepdims=False)
-    my_suffix = lax.dynamic_index_in_dim(suffix_len, req_idx, 0, keepdims=False)
-    own_owners = lax.dynamic_index_in_dim(owner_rows, req_idx, 0, keepdims=False)
-    place_limits = token_limits(own_owners, my_prefix, req_idx, n_head, n_req, chunk, slots, page_len)
-    upward = 2 * seq_idx - 1
-    origins = [head_idx]
-    for step in range(1, n_head):
-        origins += [head_idx + upward * step, head_idx - upward * step]
-    origins = jnp.stack(origins)
-    heads = jnp.arange(n_head, dtype=jnp.int32)
-    limits = jnp.sum(
-        jnp.where((origins[:, None] == heads[None, :])[:, :, None], place_limits[None], 0), axis=1
-    )
-
     positions = my_prefix + seq_idx * half_len + jnp.arange(half_len, dtype=jnp.int32)
     rows = heads_dev * half_len
     half_rope = rope_width // 2
@@ -732,52 +772,59 @@
     ]
     early_steps = [stream(first)]
     share = half_len // n_head
+    partial_value, q_turned = lax.optimization_barrier((partial_value, q_turned))
     partials = lax.all_to_all(partial_value, "head", split_axis=0, concat_axis=0, tiled=True)
-    summed = jnp.sum(partials.reshape(n_head, share, lat_width), axis=0)
-    share_t = seq_idx * half_len + head_idx * share + jnp.arange(share, dtype=jnp.int32)
-    latent = finish_latent(summed, my_prefix + share_t, share_t < my_suffix, kv_gain, latent_width)
-    copies = jnp.concatenate([latent] * n_head, axis=0)
-    fresh = lax.all_to_all(copies, "head", split_axis=0, concat_axis=0, tiled=True)
-    early_steps[0], fresh = lax.optimization_barrier((early_steps[0], fresh))
     for step in range(1, n_head - 1):
         early_steps.append(stream(early_steps[-1]))
     early_steps = [[block, None] for block in early_steps]
     for step in range(n_head - 2):
         early_steps[step][1] = swap(early_steps[step][0])
     mine = arrived[0][None] if n_req == 2 else jnp.stack(arrived)
-    mine, fresh = lax.optimization_barrier((mine, fresh))
     other = swap(mine)
     middle, late = join_pages(counts, rest, mine, other, chunk, cap, (2 * chunk, chunk))
+    middle, partials = lax.optimization_barrier((middle, partials))
+    summed = jnp.sum(partials.reshape(n_head, share, lat_width), axis=0)
+    share_t = seq_idx * half_len + head_idx * share + jnp.arange(share, dtype=jnp.int32)
+    latent = finish_latent(summed, my_prefix + share_t, share_t < live, kv_gain, latent_width)
 
     tile = 256 if rows % 256 == 0 and 256 % half_len == 0 else half_len
     shape = (tile, score_scale * math.log2(math.e), chunk, lat_width)
-    parts = {"early": (0, chunk), "middle": (chunk, 3 * chunk), "late": (3 * chunk, 4 * chunk)}
-
-    def limits_of(pieces):
-        return jnp.concatenate(
-            [limits[origin, parts[name][0] : parts[name][1]] for name, origin in pieces]
-        )
-
-    def pieces_of(name, steps):
-        return [(name, 2 * step + side + 1) for step in steps for side in range(2)]
-
-    def arrays_of(arrived_steps, steps):
-        return [arrived_steps[step][side] for step in steps for side in range(2)]
-
     last = n_head - 2
-    live = my_suffix.reshape(1)
     near_state = ()
     extra = 4 + 1 + 2 * last
     total = 1 + 2 * (last + 1) + 2 + 4 * last + extra
-    used_limits = []
+    firsts = {"early": [0], "middle": [chunk, 2 * chunk], "late": [3 * chunk]}
+    pieces = []
+
+    def piece(name, origin):
+        pieces.extend((place, origin) for place in firsts[name])
+
+    def step_pieces(name, step):
+        piece(name, 2 * step + 1)
+        piece(name, 2 * step + 2)
+
+    piece("early", 0)
+    for step in range(last + 1):
+        step_pieces("early", step)
+    piece("middle", 0)
+    for step in range(last + 1):
+        step_pieces("middle", step)
+    piece("late", 0)
+    for step in range(last + 1):
+        step_pieces("late", step)
+    limits = plan_blocks(
+        owner_rows, prefix_len, tuple(pieces), n_head, n_req, chunk, page_len
+    )
     n_blocks = 0
     state = None
 
-    def score(pieces, arrays, near=None):
+    def arrays_of(arrived_steps, steps):
+        return [arrived_steps[step][side] for step in steps for side in range(2)]
+
+    def score(arrays, near=None):
         nonlocal n_blocks, state, near_state
-        used_limits.append(limits_of(pieces))
         result = score_part(
-            n_blocks, total, used_limits[-1], q_turned, arrays, state, shape, latent_width, near
+            n_blocks, total, limits, q_turned, arrays, state, shape, latent_width, near
         )
         state = result[:5]
         near_state = result[5:] or near_state
@@ -795,62 +842,46 @@
     for step in range(last + 1):
         received = block
         if step == 0:
-            score(
-                [("early", 0)] + pieces_of("early", range(last)),
-                [first] + arrays_of(early_steps, range(last)),
-            )
+            score([first] + arrays_of(early_steps, range(last)))
         elif step == 1:
-            score(
-                pieces_of("early", [last]) + [("middle", 0)] + pieces_of("middle", [0]),
-                arrays_of(early_steps, [last]) + [middle] + arrays_of(middle_steps, [0]),
-            )
+            score(arrays_of(early_steps, [last]) + [middle] + arrays_of(middle_steps, [0]))
         else:
             score(
-                pieces_of("middle", [step - 1]),
-                arrays_of(middle_steps, [step - 1]),
-                (live, suffix_latent) if step == last else None,
+                arrays_of(middle_steps, [step - 1]), (live, suffix_latent) if step == last else None
             )
         received = tie(received)
         if step == 0:
             early_steps[last][0] = tie(early_steps[last][0])
             early_steps[last][1] = swap(early_steps[last][0])
+            most = over_groups(most)
+            received, most, latent = lax.optimization_barrier((received, most, latent))
+            copies = jnp.concatenate([latent] * n_head, axis=0)
+            fresh = lax.all_to_all(copies, "head", split_axis=0, concat_axis=0, tiled=True)
             opposite = swap(fresh)
             suffix_latent = jnp.where(
                 seq_idx == 0,
                 jnp.concatenate([fresh, opposite], axis=0),
                 jnp.concatenate([opposite, fresh], axis=0),
             )
-            most = over_groups(most)
-            received, most = lax.optimization_barrier((received, most))
-        elif step == last - 1:
-            received, suffix_latent = lax.optimization_barrier((received, suffix_latent))
         if step < last:
             block = stream(received)
         middle_steps.append([received, swap(received)])
 
-    last_pieces = pieces_of("middle", [last])
     last_arrays = arrays_of(middle_steps, [last])
 
-    known = jnp.concatenate(used_limits)
-    final = limits_of(last_pieces)
-
-    def end(blocks, blocks_limits, final_limits, final_arrays, current):
+    def end(blocks, final_arrays, current):
         return finish(
-            blocks, blocks_limits, final_limits, q_turned, current, near_state,
-            final_arrays, live, value_up_weight, half_len, shape,
+            blocks, limits, q_turned, current, near_state, final_arrays, live, value_up_weight, half_len, shape
         )
 
     def with_late(_):
         block = stream(late)
-        pieces = last_pieces + [("late", 0)]
         arrays = last_arrays + [late]
-        current, blocks, limit_list = state, n_blocks, list(used_limits)
+        current, blocks = state, n_blocks
         for step in range(last + 1):
             received = block
-            more = limits_of(pieces)
-            limit_list.append(more)
             current = score_part(
-                blocks, total, more, q_turned, arrays, current, shape, latent_width
+                blocks, total, limits, q_turned, arrays, current, shape, latent_width
             )[:5]
             blocks += sum(a.shape[0] for a in arrays) // chunk
             received, mark = lax.optimization_barrier((received, current[4]))
@@ -858,11 +889,10 @@
             if step < last:
                 block = stream(received)
             arrays = [received, swap(received)]
-            pieces = pieces_of("late", [step])
-        return end(blocks, jnp.concatenate(limit_list), limits_of(pieces), arrays, current)
+        return end(blocks, arrays, current)
 
     def without_late(_):
-        return end(n_blocks, known, final, last_arrays, state)
+        return end(n_blocks, last_arrays, state)
 
     attn_out = lax.cond(most > 2 * chunk, with_late, without_late, 0)
     new_pages = fresh.reshape(1, half_len // page_len, page_len * lat_width)

time: 125 us -> 179 us (1.43)
  waiting for transfers between devices: 13.6 us -> 32.1 us
  Pallas kernels: 46.7 us -> 63.6 us
  blocking collectives: 0 us -> 16.2 us
  starting transfers between devices: 36.7 us -> 43.7 us
  local copies, waits for them, and re-layouts: 15 us -> 9.06 us
    all_to_all x0 -> x1, blocking collectives: none -> 16.2 us  [local(): lax.all_to_all(copies, 'head', split_axis=0, concat_axis=0, tiled=True)]
    pallas_call x3 -> x6, Pallas kernels: 23.3 us -> 35.2 us  [score_part(): pl.pallas_call(functools.partial(score_kernel, shape, base, len(sources),...]
    ppermute x1, waiting for transfers between devices: 0.01 us -> 9.31 us  [local(): lax.ppermute(foreign[s - 1], 'req', [(i, (i + s) % n_req) for i in range(...]
    ppermute x6 -> x9, waiting for transfers between devices: 5.45 us -> 13.3 us  [stream(): return lax.ppermute(block, ('head', 'seq'), stream_route)]
    ppermute x6 -> x9, starting transfers between devices: 22.3 us -> 28.9 us  [stream(): return lax.ppermute(block, ('head', 'seq'), stream_route)]
    ppermute x8 -> x11, starting transfers between devices: 1.64 us -> 6.7 us  [swap(): return lax.ppermute(block, 'seq', swap_route)]
    ppermute x8 -> x11, waiting for transfers between devices: 1.61 us -> 6.19 us  [swap(): return lax.ppermute(block, 'seq', swap_route)]
    all_to_all x1 -> x0, waiting for transfers between devices: 4.39 us -> none  [local(): lax.all_to_all(copies, 'head', split_axis=0, concat_axis=0, tiled=True)]
  transfers between devices with their start and end apart: 18 -> 23, of which waited for: 5 -> 10; matrix products, arithmetic and copies ran while one was open for 12% -> 6% of each run, Pallas kernels for 23% -> 26%
where the time goes in v1:
time: 179 us; the launch traced here: 177 us
  Pallas kernels  63.6 us (36%)
  starting transfers between devices  43.7 us (24%)
  waiting for transfers between devices  32.1 us (18%)
  blocking collectives  16.2 us (9%)
  local copies, waits for them, and re-layouts  9.06 us (5%)
  other arithmetic  9.04 us (5%)
  between operations  3.03 us (2%)
    pallas_call x6, Pallas kernels, score_part(): pl.pallas_call(functools.partial(score_kernel, shape, base, len(sources),...  35.2 us
    ppermute x9, starting transfers between devices, stream(): return lax.ppermute(block, ('head', 'seq'), stream_route)  28.9 us
    all_to_all x1, blocking collectives, local(): lax.all_to_all(copies, 'head', split_axis=0, concat_axis=0, tiled=True)  16.2 us
    pallas_call x1, Pallas kernels, finish(): pl.pallas_call(functools.partial(finish_kernel, shape, depth, n_blocks, l...  13.4 us
    ppermute x9, waiting for transfers between devices, stream(): return lax.ppermute(block, ('head', 'seq'), stream_route)  13.3 us
    ppermute x1, waiting for transfers between devices, local(): lax.ppermute(foreign[s - 1], 'req', [(i, (i + s) % n_req) for i in range(...  9.31 us
    unnamed x16, local copies, waits for them, and re-layouts  7.25 us
    ppermute x11, starting transfers between devices, swap(): return lax.ppermute(block, 'seq', swap_route)  6.7 us
  transfers between devices with their start and end apart: 23, of which 10 were waited for; matrix products, arithmetic and copies ran while one was open for 6% of the time, Pallas kernels for 26%

profile of v1, /device:TPU:0, one launch (start us, length us, event | category | flops | bytes accessed | tf_op | source)
XLA Modules:
  0.0 176.9 jit_solution(11560685177557247312)
XLA Ops:
  0.6 4.9 %pick_pages.1 = (s32[2]{0:T(128)}, s32[1]{0:T(128)}, s32[1]{0:T(128)}, s32[1]{0:T(128)}, bf16[8,32,1152]{2,1,0:T(8,128)(2,1)}, /*index=5*/bf16[8,32,1152]{2,1,0:...) custom-call(s32[2,64]{1,0:T(2,128)} %bitcast.25, s32[2,64]{1,0:T(2,128)} %slot_hbm.1, s32[2]{0:T(128)} %prefix_ref.1, ...), custom_call_target="tpu_custom_call" | custom-call | flops 1000000000 | bytes 6000000 | tf_op jit(solution)/shard_map/pick_pages/pallas_call | solution.py:163
  5.6 3.0 %collective-permute-start.6 = (bf16[8,32,1152]{2,1,0:T(8,128)(2,1)}, bf16[8,32,1152]{2,1,0:T(8,128)(2,1)S(1)}, u32[]{:S(2)}, u32[]{:S(2)}) collective-permute-start(bf16[8,32,1152]{2,1,0:T(8,128)(2,1)} %bitcast.27), channel_id=1, source_target_pairs={{0,2},{2,0},{1,3},{3,1},{4,6},{6,4},{5,7},{7,5},{8,10},{10,8},{9,1... | collective-permute-start | bytes 1769480 | tf_op jit(solution)/shard_map/ppermute | solution.py:770
  8.6 3.5 %collective-permute-start.8 = (bf16[8,32,1152]{2,1,0:T(8,128)(2,1)}, bf16[8,32,1152]{2,1,0:T(8,128)(2,1)S(1)}, u32[]{:S(2)}, u32[]{:S(2)}) collective-permute-start(bf16[8,32,1152]{2,1,0:T(8,128)(2,1)} %get-tuple-element.167.refs_0_), channel_id=1, source_target_pairs={{0,4},{5,1},{4,8},{9,5},{8,12},{13,9},{2,6},{7,3},{6,10},{11,7},{1... | collective-permute-start | bytes 1769480 | tf_op jit(solution)/shard_map/ppermute | solution.py:760
  12.8 9.3 %collective-permute-done.6 = bf16[8,32,1152]{2,1,0:T(8,128)(2,1)S(1)} collective-permute-done((bf16[8,32,1152]{2,1,0:T(8,128)(2,1)}, bf16[8,32,1152]{2,1,0:T(8,128)(2,1)S(1)}, u32[]{:S(2)}, u32[]{:S(2)}) %collective-permute-start.6) | collective-permute-done | bytes 589856 | tf_op jit(solution)/shard_map/ppermute | solution.py:770
  22.1 4.6 %collective-permute-start.9 = (bf16[8,32,1152]{2,1,0:T(8,128)(2,1)S(1)}, bf16[8,32,1152]{2,1,0:T(8,128)(2,1)}, u32[]{:S(2)}, u32[]{:S(2)}) collective-permute-start(bf16[8,32,1152]{2,1,0:T(8,128)(2,1)S(1)} %collective-permute-done.8.refs_1_), channel_id=1, source_target_pairs={{0,4},{5,1},{4,8},{9,5},{8,12},{13,9},{2,6},{7,3},{6,10},{11,7},{1... | collective-permute-start | bytes 1769480 | tf_op jit(solution)/shard_map/ppermute | solution.py:760
  26.7 0.1 multiply_sine_fusion.1
  26.8 0.0 copy-start
  26.8 1.2 copy-done
  28.1 1.0 copy-done.3
  29.1 1.9 %turn_queries.1.queries_ref = bf16[640,1024]{1,0:T(8,128)(2,1)} custom-call(bf16[128,1536]{1,0:T(8,128)(2,1)S(1)} %bitcast.20, bf16[8,128,512]{2,1,0:T(8,128)(2,1)S(1)} %copy-done, f32[32,128]{1,0:T(8,128)S(1)} %get-tuple-element.207.cosine_ref, f32[32,128]{1,0:T(8,128)S(1)} %get-tuple-element.206.sine_ref), custom_call_target="tpu_custom_call" | custom-call | flops 134217728 | bytes 3000000 | tf_op jit(solution)/shard_map/turn_queries/pallas_call | solution.py:346
  31.0 3.5 %all-to-all-start = ((f32[4,32,576]{2,1,0:T(8,128)}), f32[4,32,576]{2,1,0:T(8,128)S(1)}, u32[]{:S(2)}, u32[]{:S(2)}) async-start(f32[4,32,576]{2,1,0:T(8,128)} %bitcast.24), calls=%async_computation | async-start | bytes 655360 | tf_op jit(solution)/shard_map/all_to_all | solution.py:776
  34.4 1.6 collective-permute-start.13
  36.0 1.1 copy-done.2
  37.1 0.7 copy-done.6
  37.7 4.3 %join_pages.1 = (bf16[16,32,1152]{2,1,0:T(8,128)(2,1)S(1)}, bf16[8,32,1152]{2,1,0:T(8,128)(2,1)}) custom-call(s32[2]{0:T(128)S(1)} %copy-done.6, bf16[8,32,1152]{2,1,0:T(8,128)(2,1)S(1)} %copy-done.2, bf16[1,8,32,1152]{3,2,1,0:T(8,128)(2,1)S(1)} %bitcast.19, bf16[1,8,32,1152]{3,2,1,0:T(8,128)(2,1)S(1)} %collective-permute-done.7.other_ref), custom_call_target="tpu_custom_call" | custom-call | bytes 3000000 | tf_op jit(solution)/shard_map/join_pages/pallas_call | solution.py:231
  42.1 3.3 %all-to-all-done = f32[4,32,576]{2,1,0:T(8,128)S(1)} async-done(((f32[4,32,576]{2,1,0:T(8,128)}), f32[4,32,576]{2,1,0:T(8,128)S(1)}, u32[]{:S(2)}, u32[]{:S(2)}) %all-to-all-start) | async-done | bytes 294944 | tf_op jit(solution)/shard_map/all_to_all | solution.py:776
  45.4 0.7 copy-done.10
  46.1 1.7 collective-permute-start.10
  47.8 1.2 add_convert_fusion
  49.0 3.8 %plan_blocks.1.limit_ref = s32[224]{0:T(256)S(1)} custom-call(s32[2,64]{1,0:T(2,128)} %bitcast.26, s32[2]{0:T(128)} %prefix_ref.1), custom_call_target="tpu_custom_call" | custom-call | flops 10000 | bytes 10000 | tf_op jit(solution)/shard_map/plan_blocks/pallas_call | solution.py:293
  52.8 1.2 fusion.8
  55.3 0.1 collective-permute-start.11
  55.4 1.6 reduce_sum.18
  57.1 0.5 collective-permute-start.12
  57.6 2.8 %collective-permute-start.14 = (bf16[8,32,1152]{2,1,0:T(8,128)(2,1)}, bf16[8,32,1152]{2,1,0:T(8,128)(2,1)S(1)}, u32[]{:S(2)}, u32[]{:S(2)}) collective-permute-start(bf16[8,32,1152]{2,1,0:T(8,128)(2,1)} %collective-permute-done.9.refs_3_), channel_id=1, source_target_pairs={{0,4},{5,1},{4,8},{9,5},{8,12},{13,9},{2,6},{7,3},{6,10},{11,7},{1... | collective-permute-start | bytes 1769480 | tf_op jit(solution)/shard_map/ppermute | solution.py:760
  60.4 1.0 multiply_reduce_fusion
  61.3 0.9 fusion.5
  62.3 0.9 multiply_convert_fusion
  63.2 0.8 maximum_select_fusion.1
  64.0 1.1 copy-done.1
  65.0 7.5 %score_part.9 = (f32[26,512,1024]{2,1,0:T(8,128)}, bf16[26,512,512]{2,1,0:T(8,128)(2,1)}, f32[26,1024]{1,0:T(8,128)S(1)}, f32[1,1024]{1,0:T(1,128)S(1)}, f32[1,1024]{1,0:T(1,128)S(1)}) custom-call(s32[224]{0:T(256)S(1)} %plan_blocks.1.limit_ref, bf16[640,1024]{1,0:T(8,128)(2,1)} %turn_queries.1.queries_ref, bf16[8,32,1152]{2,1,0:T(8,128)(2,1)S(1)} %copy-done.1, ...), custom_call_target="tpu_custom_call" | custom-call | flops 1310720 | bytes 100000 | tf_op jit(solution)/shard_map/score_part/pallas_call | solution.py:542
  72.5 0.1 collective-permute-start.16
  72.6 5.1 %collective-permute-start.17 = (bf16[16,32,1152]{2,1,0:T(8,128)(2,1)S(1)}, bf16[16,32,1152]{2,1,0:T(8,128)(2,1)S(1)}, u32[]{:S(2)}, u32[]{:S(2)}) collective-permute-start(bf16[16,32,1152]{2,1,0:T(8,128)(2,1)S(1)} %collective-permute-done.10.refs_8_), channel_id=1, source_target_pairs={{0,4},{5,1},{4,8},{9,5},{8,12},{13,9},{2,6},{7,3},{6,10},{11,7},{1... | collective-permute-start | bytes 3538952 | tf_op jit(solution)/shard_map/ppermute | solution.py:760
  77.8 0.1 collective-permute-start.15
  77.9 2.0 %collective-permute-done.15.refs_6_ = bf16[8,32,1152]{2,1,0:T(8,128)(2,1)S(1)} collective-permute-done((bf16[8,32,1152]{2,1,0:T(8,128)(2,1)S(1)}, bf16[8,32,1152]{2,1,0:T(8,128)(2,1)S(1)}, u32[]{:S(2)}, u32[]{:S(2)}) %collective-permute-start.15) | collective-permute-done | bytes 589856 | tf_op jit(solution)/shard_map/ppermute | solution.py:757
  79.8 9.5 %score_part.10 = (f32[26,512,1024]{2,1,0:T(8,128)}, bf16[26,512,512]{2,1,0:T(8,128)(2,1)}, f32[26,1024]{1,0:T(8,128)S(1)}, f32[1,1024]{1,0:T(1,128)S(1)}, f32[1,1024]{1,0:T(1,128)S(1)}) custom-call(s32[224]{0:T(256)S(1)} %plan_blocks.1.limit_ref, bf16[640,1024]{1,0:T(8,128)(2,1)} %turn_queries.1.queries_ref, ...), custom_call_target="tpu_custom_call", output_to_operand_aliasing={{0}: (5, {}), {1}: (6, {})} | custom-call | flops 2097152 | bytes 100000 | tf_op jit(solution)/shard_map/score_part/pallas_call | solution.py:542
  89.3 0.6 copy-done.4
  90.0 1.4 collective-permute-done.17.refs_7_
  91.4 0.1 collective-permute-start.19
  91.5 4.4 %collective-permute-start.20 = (bf16[16,32,1152]{2,1,0:T(8,128)(2,1)S(1)}, bf16[16,32,1152]{2,1,0:T(8,128)(2,1)S(1)}, u32[]{:S(2)}, u32[]{:S(2)}) collective-permute-start(bf16[16,32,1152]{2,1,0:T(8,128)(2,1)S(1)} %collective-permute-done.17.refs_7_), channel_id=1, source_target_pairs={{0,4},{5,1},{4,8},{9,5},{8,12},{13,9},{2,6},{7,3},{6,10},{11,7},{1... | collective-permute-start | bytes 3538952 | tf_op jit(solution)/shard_map/ppermute | solution.py:760
  95.9 16.2 %all_to_all.24 = bf16[4,32,576]{2,1,0:T(8,128)(2,1)} all-to-all(bf16[4,32,576]{2,1,0:T(8,128)(2,1)S(1)} %bitcast.22), channel_id=1, replica_groups=mesh['groups'=2,'head'=4,'req'=2,'seq'=2] {'head'}, dimensions={0} | all-to-all | bytes 294912 | tf_op jit(solution)/shard_map/all_to_all | solution.py:859
  112.1 2.3 %collective-permute-start.18 = (bf16[128,576]{1,0:T(8,128)(2,1)}, bf16[128,576]{1,0:T(8,128)(2,1)}, u32[]{:S(2)}, u32[]{:S(2)}) collective-permute-start(bf16[128,576]{1,0:T(8,128)(2,1)} %bitcast.17), channel_id=1, source_target_pairs={{0,1},{1,0},{2,3},{3,2},{4,5},{5,4},{6,7},{7,6},{8,9},{9,8},{10,11... | collective-permute-start | bytes 442376 | tf_op jit(solution)/shard_map/ppermute | solution.py:757
  114.4 1.4 collective-permute-done.18
  115.7 1.2 maximum_select_fusion.refs_6_
  117.0 0.9 copy-done.5
  117.9 7.9 %score_part.11 = (f32[26,512,1024]{2,1,0:T(8,128)}, bf16[26,512,512]{2,1,0:T(8,128)(2,1)}, f32[26,1024]{1,0:T(8,128)}, f32[1,1024]{1,0:T(1,128)S(1)}, f32[1,1024...) custom-call(s32[224]{0:T(256)S(1)} %plan_blocks.1.limit_ref, ...), custom_call_target="tpu_custom_call", output_to_operand_aliasing={{0}: (5, {}), {1}: (6, {})} | custom-call | flops 1048576 | bytes 100000 | tf_op jit(solution)/shard_map/score_part/pallas_call | solution.py:542
  125.8 0.3 collective-permute-start.21
  126.1 1.8 %reshape.49 = bf16[1,2,36864]{2,1,0:T(2,128)(2,1)} reshape(bf16[4,32,576]{2,1,0:T(8,128)(2,1)} %all_to_all.24) | data formatting | bytes 294912 | tf_op jit(solution)/shard_map/reshape | solution.py:898
  127.9 0.9 collective-permute-done.21
  128.8 47.9 %conditional.1 = (bf16[1,128,1024]{2,1,0:T(8,128)(2,1)}) conditional(s32[]{:T(128)} %convert_element_type.20, (s32[224]{0:T(256)S(1)}, bf16[640,1024]{1,0:T(8,128)(2,1)}, f32[26,1024]{1,0:T(8,128)}, f32[1,1024]{1,0:T(1,128)S(1)}, f32[1,1024]{1,0:T(1,128)}, /*index=5*/f32[256,1024]{1,0:T(8,128)}, bf16[512,256]{1,0:T(8,128)(2,1)}, f32[1,1024]{1,0:T(1,128)}, ...), branch_computations={%region_2.3_spmd, %region_3.4_spmd} | conditional | flops 8055422976 | bytes 59152612 | solution.py:897
  128.8 1.3 collective-permute-start
  130.2 5.7 %score_part.6 = (f32[26,512,1024]{2,1,0:T(8,128)}, bf16[26,512,512]{2,1,0:T(8,128)(2,1)}, f32[26,1024]{1,0:T(8,128)S(1)}, f32[1,1024]{1,0:T(1,128)S(1)}, f32[1,1024]{1,0:T(1,128)S(1)}) custom-call(s32[224]{0:T(256)S(1)} %get-tuple-element.76.limit_ref, ...), custom_call_target="tpu_custom_call", output_to_operand_aliasing={{0}: (5, {}), {1}: (6, {})} | custom-call | flops 1310720 | bytes 100000 | tf_op jit(solution)/shard_map/cond/branch_1_fun/score_part/pallas_call | solution.py:542
  135.9 1.9 %collective-permute-done.refs_5_ = bf16[8,32,1152]{2,1,0:T(8,128)(2,1)S(1)} collective-permute-done((bf16[8,32,1152]{2,1,0:T(8,128)(2,1)}, bf16[8,32,1152]{2,1,0:T(8,128)(2,1)S(1)}, u32[]{:S(2)}, u32[]{:S(2)}) %collective-permute-start) | collective-permute-done | bytes 589856 | tf_op jit(solution)/shard_map/cond/branch_1_fun/ppermute | solution.py:760
  137.8 2.1 %collective-permute-start.1 = (bf16[8,32,1152]{2,1,0:T(8,128)(2,1)S(1)}, bf16[8,32,1152]{2,1,0:T(8,128)(2,1)S(1)}, u32[]{:S(2)}, u32[]{:S(2)}) collective-permute-start(bf16[8,32,1152]{2,1,0:T(8,128)(2,1)S(1)} %collective-permute-done.refs_5_), channel_id=1, source_target_pairs={{0,1},{1,0},{2,3},{3,2},{4,5},{5,4},{6,7},{7,6},{8,9},{9,8},{10,11... | collective-permute-start | bytes 1769480 | tf_op jit(solution)/shard_map/cond/branch_1_fun/ppermute | solution.py:757
  139.9 2.2 %collective-permute-start.2 = (bf16[8,32,1152]{2,1,0:T(8,128)(2,1)S(1)}, bf16[8,32,1152]{2,1,0:T(8,128)(2,1)S(1)}, u32[]{:S(2)}, u32[]{:S(2)}) collective-permute-start(bf16[8,32,1152]{2,1,0:T(8,128)(2,1)S(1)} %collective-permute-done.refs_5_), channel_id=1, source_target_pairs={{0,4},{5,1},{4,8},{9,5},{8,12},{13,9},{2,6},{7,3},{6,10},{11,7},{1... | collective-permute-start | bytes 1769480 | tf_op jit(solution)/shard_map/cond/branch_1_fun/ppermute | solution.py:760
  142.2 1.0 score_part.7
  143.1 6.4 %collective-permute-done.2.refs_5_ = bf16[8,32,1152]{2,1,0:T(8,128)(2,1)S(1)} collective-permute-done((bf16[8,32,1152]{2,1,0:T(8,128)(2,1)S(1)}, bf16[8,32,1152]{2,1,0:T(8,128)(2,1)S(1)}, u32[]{:S(2)}, u32[]{:S(2)}) %collective-permute-start.2) | collective-permute-done | bytes 589856 | tf_op jit(solution)/shard_map/cond/branch_1_fun/ppermute | solution.py:760
  149.5 1.1 collective-permute-start.3
  150.6 3.3 %collective-permute-start.4 = (bf16[8,32,1152]{2,1,0:T(8,128)(2,1)S(1)}, bf16[8,32,1152]{2,1,0:T(8,128)(2,1)S(1)}, u32[]{:S(2)}, u32[]{:S(2)}) collective-permute-start(bf16[8,32,1152]{2,1,0:T(8,128)(2,1)S(1)} %collective-permute-done.2.refs_5_), channel_id=1, source_target_pairs={{0,4},{5,1},{4,8},{9,5},{8,12},{13,9},{2,6},{7,3},{6,10},{11,7},{1... | collective-permute-start | bytes 1769480 | tf_op jit(solution)/shard_map/cond/branch_1_fun/ppermute | solution.py:760
  154.0 3.7 %score_part.8 = (f32[26,512,1024]{2,1,0:T(8,128)}, bf16[26,512,512]{2,1,0:T(8,128)(2,1)}, f32[26,1024]{1,0:T(8,128)S(1)}, f32[1,1024]{1,0:T(1,128)S(1)}, f32[1,1024]{1,0:T(1,128)S(1)}) custom-call(s32[224]{0:T(256)S(1)} %get-tuple-element.76.limit_ref, bf16[640,1024]{1,0:T(8,128)(2,1)S(1)} %copy-done.7, ...), custom_call_target="tpu_custom_call", output_to_operand_aliasing={{0}: (5, {}), {1}: (6, {})} | custom-call | flops 524288 | bytes 100000 | tf_op jit(solution)/shard_map/cond/branch_1_fun/score_part/pallas_call | solution.py:542
  157.7 3.6 %collective-permute-done.4.refs_0_ = bf16[8,32,1152]{2,1,0:T(8,128)(2,1)S(1)} collective-permute-done((bf16[8,32,1152]{2,1,0:T(8,128)(2,1)S(1)}, bf16[8,32,1152]{2,1,0:T(8,128)(2,1)S(1)}, u32[]{:S(2)}, u32[]{:S(2)}) %collective-permute-start.4) | collective-permute-done | bytes 589856 | tf_op jit(solution)/shard_map/cond/branch_1_fun/ppermute | solution.py:760
  161.3 0.1 collective-permute-start.5
  161.4 1.9 %collective-permute-done.5.refs_1_ = bf16[8,32,1152]{2,1,0:T(8,128)(2,1)S(1)} collective-permute-done((bf16[8,32,1152]{2,1,0:T(8,128)(2,1)S(1)}, bf16[8,32,1152]{2,1,0:T(8,128)(2,1)S(1)}, u32[]{:S(2)}, u32[]{:S(2)}) %collective-permute-start.5) | collective-permute-done | bytes 589856 | tf_op jit(solution)/shard_map/cond/branch_1_fun/ppermute | solution.py:757
  163.3 13.4 %finish.3 = bf16[128,1024]{1,0:T(8,128)(2,1)} custom-call(s32[224]{0:T(256)S(1)} %get-tuple-element.76.limit_ref, bf16[640,1024]{1,0:T(8,128)(2,1)S(1)} %copy-done.7, f32[26,1024]{1,0:T(8,128)S(1)} %get-tuple-element.100.marks, f32[1,1024]{1,0:T(1,128)S(1)} %get-tuple-element.101.sum_in, f32[1,1024]{1,0:T(1,128)S(1)} %get-tuple-element.103.high_in, ...), custom_call_target="tpu_custom_call" | custom-call | flops 8053063680 | bytes 30000000 | tf_op jit(solution)/shard_map/cond/branch_1_fun/finish/pallas_call | solution.py:678
  (35 shorter events, 0.1 us)
Async XLA Ops:
  5.6 16.5 %collective-permute-start.6 = (bf16[8,32,1152]{2,1,0:T(8,128)(2,1)}, bf16[8,32,1152]{2,1,0:T(8,128)(2,1)S(1)}, u32[]{:S(2)}, u32[]{:S(2)}) collective-permute-start(bf16[8,32,1152]{2,1,0:T(8,128)(2,1)} %bitcast.27), channel_id=1, source_target_pairs={{0,2},{2,0},{1,3},{3,1},{4,6},{6,4},{5,7},{7,5},{8,10},{10,8},{9,1... | collective-permute-start | bytes 1769480 | tf_op jit(solution)/shard_map/ppermute | solution.py:770
  8.6 13.5 %collective-permute-start.8 = (bf16[8,32,1152]{2,1,0:T(8,128)(2,1)}, bf16[8,32,1152]{2,1,0:T(8,128)(2,1)S(1)}, u32[]{:S(2)}, u32[]{:S(2)}) collective-permute-start(bf16[8,32,1152]{2,1,0:T(8,128)(2,1)} %get-tuple-element.167.refs_0_), channel_id=1, source_target_pairs={{0,4},{5,1},{4,8},{9,5},{8,12},{13,9},{2,6},{7,3},{6,10},{11,7},{1... | collective-permute-start | bytes 1769480 | tf_op jit(solution)/shard_map/ppermute | solution.py:760
  22.1 13.9 %collective-permute-start.7 = (bf16[1,8,32,1152]{3,2,1,0:T(8,128)(2,1)S(1)}, bf16[1,8,32,1152]{3,2,1,0:T(8,128)(2,1)S(1)}, u32[]{:S(2)}, u32[]{:S(2)}) collective-permute-start(bf16[1,8,32,1152]{3,2,1,0:T(8,128)(2,1)S(1)} %bitcast.18), channel_id=1, source_target_pairs={{0,1},{1,0},{2,3},{3,2},{4,5},{5,4},{6,7},{7,6},{8,9},{9,8},{10,11... | collective-permute-start | bytes 1769480 | tf_op jit(solution)/shard_map/ppermute | solution.py:757
  22.1 24.0 %collective-permute-start.9 = (bf16[8,32,1152]{2,1,0:T(8,128)(2,1)S(1)}, bf16[8,32,1152]{2,1,0:T(8,128)(2,1)}, u32[]{:S(2)}, u32[]{:S(2)}) collective-permute-start(bf16[8,32,1152]{2,1,0:T(8,128)(2,1)S(1)} %collective-permute-done.8.refs_1_), channel_id=1, source_target_pairs={{0,4},{5,1},{4,8},{9,5},{8,12},{13,9},{2,6},{7,3},{6,10},{11,7},{1... | collective-permute-start | bytes 1769480 | tf_op jit(solution)/shard_map/ppermute | solution.py:760
  26.8 1.2 copy-start
  28.1 1.0 copy-start.3
  31.0 14.4 %all-to-all-start = ((f32[4,32,576]{2,1,0:T(8,128)}), f32[4,32,576]{2,1,0:T(8,128)S(1)}, u32[]{:S(2)}, u32[]{:S(2)}) async-start(f32[4,32,576]{2,1,0:T(8,128)} %bitcast.24), calls=%async_computation | async-start | bytes 655360 | tf_op jit(solution)/shard_map/all_to_all | solution.py:776
  34.4 19.6 %collective-permute-start.13 = (s32[1]{0:T(128)}, s32[1]{0:T(128)}, u32[]{:S(2)}, u32[]{:S(2)}) collective-permute-start(s32[1]{0:T(128)} %get-tuple-element.173), channel_id=1, source_target_pairs={{0,16},{16,0},{1,17},{17,1},{2,18},{18,2},{3,19},{19,3},{4,20},{20... | collective-permute-start | bytes 20 | tf_op jit(solution)/shard_map/ppermute | solution.py:312
  36.0 1.1 copy-start.2
  37.1 0.7 copy-start.6
  45.4 0.7 copy-start.10
  46.1 26.4 %collective-permute-start.10 = (bf16[16,32,1152]{2,1,0:T(8,128)(2,1)S(1)}, bf16[16,32,1152]{2,1,0:T(8,128)(2,1)S(1)}, u32[]{:S(2)}, u32[]{:S(2)}) collective-permute-start(bf16[16,32,1152]{2,1,0:T(8,128)(2,1)S(1)} %get-tuple-element.168.refs_7_), channel_id=1, source_target_pairs={{0,4},{5,1},{4,8},{9,5},{8,12},{13,9},{2,6},{7,3},{6,10},{11,7},{1... | collective-permute-start | bytes 3538952 | tf_op jit(solution)/shard_map/ppermute | solution.py:760
  55.3 8.6 %collective-permute-start.11 = (bf16[8,32,1152]{2,1,0:T(8,128)(2,1)S(1)}, bf16[8,32,1152]{2,1,0:T(8,128)(2,1)S(1)}, u32[]{:S(2)}, u32[]{:S(2)}) collective-permute-start(bf16[8,32,1152]{2,1,0:T(8,128)(2,1)S(1)} %collective-permute-done.8.refs_1_), channel_id=1, source_target_pairs={{0,1},{1,0},{2,3},{3,2},{4,5},{5,4},{6,7},{7,6},{8,9},{9,8},{10,11... | collective-permute-start | bytes 1769480 | tf_op jit(solution)/shard_map/ppermute | solution.py:757
  57.1 6.9 %collective-permute-start.12 = (bf16[8,32,1152]{2,1,0:T(8,128)(2,1)}, bf16[8,32,1152]{2,1,0:T(8,128)(2,1)S(1)}, u32[]{:S(2)}, u32[]{:S(2)}) collective-permute-start(bf16[8,32,1152]{2,1,0:T(8,128)(2,1)} %collective-permute-done.9.refs_3_), channel_id=1, source_target_pairs={{0,1},{1,0},{2,3},{3,2},{4,5},{5,4},{6,7},{7,6},{8,9},{9,8},{10,11... | collective-permute-start | bytes 1769480 | tf_op jit(solution)/shard_map/ppermute | solution.py:757
  57.6 20.2 %collective-permute-start.14 = (bf16[8,32,1152]{2,1,0:T(8,128)(2,1)}, bf16[8,32,1152]{2,1,0:T(8,128)(2,1)S(1)}, u32[]{:S(2)}, u32[]{:S(2)}) collective-permute-start(bf16[8,32,1152]{2,1,0:T(8,128)(2,1)} %collective-permute-done.9.refs_3_), channel_id=1, source_target_pairs={{0,4},{5,1},{4,8},{9,5},{8,12},{13,9},{2,6},{7,3},{6,10},{11,7},{1... | collective-permute-start | bytes 1769480 | tf_op jit(solution)/shard_map/ppermute | solution.py:760
  64.0 1.1 copy-start.1
  72.5 7.3 %collective-permute-start.16 = (bf16[16,32,1152]{2,1,0:T(8,128)(2,1)S(1)}, bf16[16,32,1152]{2,1,0:T(8,128)(2,1)S(1)}, u32[]{:S(2)}, u32[]{:S(2)}) collective-permute-start(bf16[16,32,1152]{2,1,0:T(8,128)(2,1)S(1)} %collective-permute-done.10.refs_8_), channel_id=1, source_target_pairs={{0,1},{1,0},{2,3},{3,2},{4,5},{5,4},{6,7},{7,6},{8,9},{9,8},{10,11... | collective-permute-start | bytes 3538952 | tf_op jit(solution)/shard_map/ppermute | solution.py:757
  72.6 18.8 %collective-permute-start.17 = (bf16[16,32,1152]{2,1,0:T(8,128)(2,1)S(1)}, bf16[16,32,1152]{2,1,0:T(8,128)(2,1)S(1)}, u32[]{:S(2)}, u32[]{:S(2)}) collective-permute-start(bf16[16,32,1152]{2,1,0:T(8,128)(2,1)S(1)} %collective-permute-done.10.refs_8_), channel_id=1, source_target_pairs={{0,4},{5,1},{4,8},{9,5},{8,12},{13,9},{2,6},{7,3},{6,10},{11,7},{1... | collective-permute-start | bytes 3538952 | tf_op jit(solution)/shard_map/ppermute | solution.py:760
  77.8 2.1 %collective-permute-start.15 = (bf16[8,32,1152]{2,1,0:T(8,128)(2,1)S(1)}, bf16[8,32,1152]{2,1,0:T(8,128)(2,1)S(1)}, u32[]{:S(2)}, u32[]{:S(2)}) collective-permute-start(bf16[8,32,1152]{2,1,0:T(8,128)(2,1)S(1)} %collective-permute-done.14.refs_5_), channel_id=1, source_target_pairs={{0,1},{1,0},{2,3},{3,2},{4,5},{5,4},{6,7},{7,6},{8,9},{9,8},{10,11... | collective-permute-start | bytes 1769480 | tf_op jit(solution)/shard_map/ppermute | solution.py:757
  89.3 0.7 copy-start.4
  91.4 25.6 %collective-permute-start.19 = (bf16[16,32,1152]{2,1,0:T(8,128)(2,1)S(1)}, bf16[16,32,1152]{2,1,0:T(8,128)(2,1)S(1)}, u32[]{:S(2)}, u32[]{:S(2)}) collective-permute-start(bf16[16,32,1152]{2,1,0:T(8,128)(2,1)S(1)} %collective-permute-done.17.refs_7_), channel_id=1, source_target_pairs={{0,1},{1,0},{2,3},{3,2},{4,5},{5,4},{6,7},{7,6},{8,9},{9,8},{10,11... | collective-permute-start | bytes 3538952 | tf_op jit(solution)/shard_map/ppermute | solution.py:757
  91.5 34.3 %collective-permute-start.20 = (bf16[16,32,1152]{2,1,0:T(8,128)(2,1)S(1)}, bf16[16,32,1152]{2,1,0:T(8,128)(2,1)S(1)}, u32[]{:S(2)}, u32[]{:S(2)}) collective-permute-start(bf16[16,32,1152]{2,1,0:T(8,128)(2,1)S(1)} %collective-permute-done.17.refs_7_), channel_id=1, source_target_pairs={{0,4},{5,1},{4,8},{9,5},{8,12},{13,9},{2,6},{7,3},{6,10},{11,7},{1... | collective-permute-start | bytes 3538952 | tf_op jit(solution)/shard_map/ppermute | solution.py:760
  112.1 3.6 %collective-permute-start.18 = (bf16[128,576]{1,0:T(8,128)(2,1)}, bf16[128,576]{1,0:T(8,128)(2,1)}, u32[]{:S(2)}, u32[]{:S(2)}) collective-permute-start(bf16[128,576]{1,0:T(8,128)(2,1)} %bitcast.17), channel_id=1, source_target_pairs={{0,1},{1,0},{2,3},{3,2},{4,5},{5,4},{6,7},{7,6},{8,9},{9,8},{10,11... | collective-permute-start | bytes 442376 | tf_op jit(solution)/shard_map/ppermute | solution.py:757
  117.0 0.9 copy-start.5
  125.8 3.0 %collective-permute-start.21 = (bf16[16,32,1152]{2,1,0:T(8,128)(2,1)S(1)}, bf16[16,32,1152]{2,1,0:T(8,128)(2,1)}, u32[]{:S(2)}, u32[]{:S(2)}) collective-permute-start(bf16[16,32,1152]{2,1,0:T(8,128)(2,1)S(1)} %collective-permute-done.20), channel_id=1, source_target_pairs={{0,1},{1,0},{2,3},{3,2},{4,5},{5,4},{6,7},{7,6},{8,9},{9,8},{10,11... | collective-permute-start | bytes 3538952 | tf_op jit(solution)/shard_map/ppermute | solution.py:757
  128.8 9.0 %collective-permute-start = (bf16[8,32,1152]{2,1,0:T(8,128)(2,1)}, bf16[8,32,1152]{2,1,0:T(8,128)(2,1)S(1)}, u32[]{:S(2)}, u32[]{:S(2)}) collective-permute-start(bf16[8,32,1152]{2,1,0:T(8,128)(2,1)} %get-tuple-element.85.refs_7_), channel_id=1, source_target_pairs={{0,4},{5,1},{4,8},{9,5},{8,12},{13,9},{2,6},{7,3},{6,10},{11,7},{1... | collective-permute-start | bytes 1769480 | tf_op jit(solution)/shard_map/cond/branch_1_fun/ppermute | solution.py:760
  130.2 12.0 %copy-start.7 = (bf16[640,1024]{1,0:T(8,128)(2,1)S(1)}, bf16[640,1024]{1,0:T(8,128)(2,1)}, u32[]{:S(2)}) copy-start(bf16[640,1024]{1,0:T(8,128)(2,1)} %get-tuple-element.77.queries_ref) | copy-start | bytes 3932164 | tf_op jit(solution)/shard_map/cond
  137.8 4.3 %collective-permute-start.1 = (bf16[8,32,1152]{2,1,0:T(8,128)(2,1)S(1)}, bf16[8,32,1152]{2,1,0:T(8,128)(2,1)S(1)}, u32[]{:S(2)}, u32[]{:S(2)}) collective-permute-start(bf16[8,32,1152]{2,1,0:T(8,128)(2,1)S(1)} %collective-permute-done.refs_5_), channel_id=1, source_target_pairs={{0,1},{1,0},{2,3},{3,2},{4,5},{5,4},{6,7},{7,6},{8,9},{9,8},{10,11... | collective-permute-start | bytes 1769480 | tf_op jit(solution)/shard_map/cond/branch_1_fun/ppermute | solution.py:757
  139.9 9.5 %collective-permute-start.2 = (bf16[8,32,1152]{2,1,0:T(8,128)(2,1)S(1)}, bf16[8,32,1152]{2,1,0:T(8,128)(2,1)S(1)}, u32[]{:S(2)}, u32[]{:S(2)}) collective-permute-start(bf16[8,32,1152]{2,1,0:T(8,128)(2,1)S(1)} %collective-permute-done.refs_5_), channel_id=1, source_target_pairs={{0,4},{5,1},{4,8},{9,5},{8,12},{13,9},{2,6},{7,3},{6,10},{11,7},{1... | collective-permute-start | bytes 1769480 | tf_op jit(solution)/shard_map/cond/branch_1_fun/ppermute | solution.py:760
  149.5 4.4 %collective-permute-start.3 = (bf16[8,32,1152]{2,1,0:T(8,128)(2,1)S(1)}, bf16[8,32,1152]{2,1,0:T(8,128)(2,1)S(1)}, u32[]{:S(2)}, u32[]{:S(2)}) collective-permute-start(bf16[8,32,1152]{2,1,0:T(8,128)(2,1)S(1)} %collective-permute-done.2.refs_5_), channel_id=1, source_target_pairs={{0,1},{1,0},{2,3},{3,2},{4,5},{5,4},{6,7},{7,6},{8,9},{9,8},{10,11... | collective-permute-start | bytes 1769480 | tf_op jit(solution)/shard_map/cond/branch_1_fun/ppermute | solution.py:757
  150.6 10.7 %collective-permute-start.4 = (bf16[8,32,1152]{2,1,0:T(8,128)(2,1)S(1)}, bf16[8,32,1152]{2,1,0:T(8,128)(2,1)S(1)}, u32[]{:S(2)}, u32[]{:S(2)}) collective-permute-start(bf16[8,32,1152]{2,1,0:T(8,128)(2,1)S(1)} %collective-permute-done.2.refs_5_), channel_id=1, source_target_pairs={{0,4},{5,1},{4,8},{9,5},{8,12},{13,9},{2,6},{7,3},{6,10},{11,7},{1... | collective-permute-start | bytes 1769480 | tf_op jit(solution)/shard_map/cond/branch_1_fun/ppermute | solution.py:760
  153.9 9.3 %copy-start.8 = (bf16[8,512,128]{2,1,0:T(8,128)(2,1)S(1)}, bf16[8,512,128]{2,1,0:T(8,128)(2,1)}, u32[]{:S(2)}) copy-start(bf16[8,512,128]{2,1,0:T(8,128)(2,1)} %get-tuple-element.108.up_ref) | copy-start | bytes 3145732 | tf_op jit(solution)/shard_map/cond
  153.9 9.3 %copy-start.9 = (f32[256,1024]{1,0:T(8,128)S(1)}, f32[256,1024]{1,0:T(8,128)}, u32[]{:S(2)}) copy-start(f32[256,1024]{1,0:T(8,128)} %get-tuple-element.104.near_weights) | copy-start | bytes 3145732 | tf_op jit(solution)/shard_map/cond
  153.9 9.3 %copy-start.11 = (bf16[512,256]{1,0:T(8,128)(2,1)S(1)}, bf16[512,256]{1,0:T(8,128)(2,1)}, u32[]{:S(2)}) copy-start(bf16[512,256]{1,0:T(8,128)(2,1)} %get-tuple-element.105.near_values) | copy-start | bytes 786436 | tf_op jit(solution)/shard_map/cond
  154.0 9.3 %copy-start.12 = (f32[1,1024]{1,0:T(1,128)S(1)}, f32[1,1024]{1,0:T(1,128)}, u32[]{:S(2)}) copy-start(f32[1,1024]{1,0:T(1,128)} %get-tuple-element.106.near_mark) | copy-start | bytes 12292 | tf_op jit(solution)/shard_map/cond
  161.3 2.0 %collective-permute-start.5 = (bf16[8,32,1152]{2,1,0:T(8,128)(2,1)S(1)}, bf16[8,32,1152]{2,1,0:T(8,128)(2,1)S(1)}, u32[]{:S(2)}, u32[]{:S(2)}) collective-permute-start(bf16[8,32,1152]{2,1,0:T(8,128)(2,1)S(1)} %collective-permute-done.4.refs_0_), channel_id=1, source_target_pairs={{0,1},{1,0},{2,3},{3,2},{4,5},{5,4},{6,7},{7,6},{8,9},{9,8},{10,11... | collective-permute-start | bytes 1769480 | tf_op jit(solution)/shard_map/cond/branch_1_fun/ppermute | solution.py:757
